TPU v7x, 128 devices: a whole 4x4x4 slice. The times are simulated.
128 devices in a mesh: region: 4 (over z), dev: 32 (over y, x, core).
Axes of the slice: x: 4, y: 4, z: 4, core: 2. Of those that a mesh axis runs over, the one named last changes fastest.
Arguments:
- states: bfloat16 [32768, 512], P(('region', 'dev')), may hold values from -6 to 6
- norm_gain: float32 [512], replicated, may hold values from 0.1 to 1.9
- w_query: bfloat16 [512, 512], replicated, may hold values from -0.25 to 0.25
- w_key: bfloat16 [512, 512], replicated, may hold values from -0.25 to 0.25
- w_value: bfloat16 [512, 512], replicated, may hold values from -1 to 1
- w_out: bfloat16 [512, 512], replicated, may hold values from -0.25 to 0.25
- neighbours: int32 [256, 6], P(('region', 'dev')), may hold values from 0 to 255, as said below
- labels: int32 [256, 128], P(('region', 'dev')), may hold values from 0 to 3
- cotangent: bfloat16 [32768, 512], P(('region', 'dev')), may hold values from -6 to 6
Outputs:
- branch_out: bfloat16 [32768, 512], P(('region', 'dev'))
- grad_states: bfloat16 [32768, 512], P(('region', 'dev'))
- grad_query: float32 [512, 512], replicated
- grad_key: float32 [512, 512], replicated
- grad_value: float32 [512, 512], replicated
- grad_output: float32 [512, 512], replicated
- grad_gain: float32 [512], replicated
Inputs may be any that keep to these rules, and one draw needn't show every extreme that they name: `neighbours`: blocks are numbered device by device, region group first, then dev index, 2 to a device. Entry 0 of row b is b itself. Entries 1 to 4 lie on devices of b's own region group; over the 2 blocks of one device these 8 entries name distinct blocks, at most 1 of them on any one device, and exactly 1 on some device. Entry 5 lies in the next region group (the last group's next is the first) at the same dev index, and the entries 5 of one device's blocks name each block of that device once.
All inputs are finite; a program needn't handle non-finite values.
Results may differ from a plain program's by a relative error of at most 0.015.
Values may be sent and summed in bfloat16 or wider, within the bound.
A program may use at most 128 MiB of HBM per device.

v0:
```python
import math

import jax
import jax.numpy as jnp
from jax import lax
from jax.sharding import PartitionSpec as P

HEADS = 8


EPSILON = 1e-05


def shortened(array):
    return jax.tree.map(lambda a: a.astype(jnp.bfloat16) if a.dtype == jnp.float32 else a, array)


def passed_along(value, axis, steps):
    count = lax.axis_size(axis)
    pairs = [(source, (source + steps) % count) for source in range(count)]
    return lax.ppermute(value, axis, pairs)


def normalize(row_block, norm_gain):
    widened = row_block.astype(jnp.float32)
    inverse = lax.rsqrt(jnp.mean(widened * widened, axis=-1, keepdims=True) + EPSILON)
    return ((widened * inverse * norm_gain).astype(jnp.bfloat16), inverse)


def normalize_back(row_block, norm_gain, inverse, d_normed):
    widened = row_block.astype(jnp.float32)
    grad_gain = jnp.sum(d_normed * widened * inverse, axis=0)
    along_rows = (
        jnp.sum(d_normed * norm_gain * widened, axis=-1, keepdims=True) / row_block.shape[-1]
    )
    grad_rows = inverse * norm_gain * d_normed - widened * inverse * inverse * inverse * along_rows
    return (grad_gain, grad_rows.astype(jnp.bfloat16))


def project(row_block, weight):
    return jnp.dot(row_block, weight, preferred_element_type=jnp.float32).astype(jnp.bfloat16)


def pair_terms(normed_rows, pair_rows, w_key, w_value):
    model_width = normed_rows.shape[-1]
    flat_normed = normed_rows.reshape(-1, model_width)
    flat_pairs = pair_rows.reshape(-1, 2 * model_width)
    grad_pairs = jnp.einsum(
        "rd,re->de", flat_normed, flat_pairs, preferred_element_type=jnp.float32
    )
    parts = jnp.einsum(
        "re,de->rd", flat_pairs[:, :model_width], w_key, preferred_element_type=jnp.float32
    )
    parts = parts + jnp.einsum(
        "re,de->rd", flat_pairs[:, model_width:], w_value, preferred_element_type=jnp.float32
    )
    parts = parts.astype(jnp.bfloat16).reshape(pair_rows.shape[:-1] + (model_width,))
    return (grad_pairs, parts)


def attend(query_block, keyval, allowed):
    model_width = query_block.shape[-1]
    head_dim = model_width // HEADS
    query_count = query_block.shape[0]
    key_pairs = keyval.reshape(-1, 2 * model_width)
    key_count = key_pairs.shape[0]
    query_heads = query_block.reshape(query_count, HEADS, head_dim)
    key_heads = key_pairs[:, :model_width].reshape(key_count, HEADS, head_dim)
    value_heads = key_pairs[:, model_width:].reshape(key_count, HEADS, head_dim)
    scores = jnp.einsum(
        "qhd,khd->hqk", query_heads, key_heads, preferred_element_type=jnp.float32
    ) / math.sqrt(head_dim)
    weights = jnp.where(allowed[None], jnp.exp(scores), 0.0)
    probabilities = (weights / jnp.sum(weights, axis=-1, keepdims=True)).astype(jnp.bfloat16)
    mixture = jnp.einsum(
        "hqk,khd->qhd", probabilities, value_heads, preferred_element_type=jnp.float32
    )
    return mixture.reshape(query_count, model_width).astype(jnp.bfloat16)


def across_dev(parcel):
    return jax.tree.map(
        lambda part, own: part.astype(own.dtype),
        lax.all_to_all(shortened(parcel), "dev", split_axis=0, concat_axis=0, tiled=True),
        parcel,
    )


def across_region(parcel, offset):
    return jax.tree.map(
        lambda part, own: part.astype(own.dtype),
        passed_along(shortened(parcel), "region", offset),
        parcel,
    )


def body(states, norm_gain, w_query, w_key, w_value, w_out, neighbours, labels, cotangent):
    dev_count = lax.axis_size("dev")
    region_count = lax.axis_size("region")
    block_count, block_rows = labels.shape
    model_width = states.shape[1]
    per_peer = max(1, 4 * block_count // dev_count)
    slot_total = dev_count * per_peer
    group_size = math.gcd(block_count, 4)
    state_total = states.shape[0] * dev_count * region_count
    normed, inverse = normalize(states, norm_gain)
    queries = project(normed, w_query)
    key_rows = project(normed, w_key)
    value_rows = project(normed, w_value)
    keyval_own = jnp.concatenate([key_rows, value_rows], axis=-1).reshape(
        block_count, block_rows, 2 * model_width
    )
    normed_blocks = normed.reshape(block_count, block_rows, model_width)
    inside = neighbours[:, 1:5].reshape(-1)
    request_count = inside.shape[0]
    owners = inside // block_count % dev_count
    local_ids = inside % block_count
    positions = jnp.arange(request_count, dtype=jnp.int32)
    earlier = (owners[:, None] == owners[None, :]) & (positions[None, :] < positions[:, None])
    slot_number = owners * per_peer + jnp.sum(earlier.astype(jnp.int32), axis=1)
    slot_hits = slot_number[:, None] == jnp.arange(slot_total, dtype=jnp.int32)[None, :]
    request = jnp.sum(jnp.where(slot_hits, local_ids[:, None] + 1, 0), axis=0) - 1
    asked_for = lax.all_to_all(
        request.reshape(dev_count, per_peer), "dev", split_axis=0, concat_axis=0, tiled=True
    )
    served = jnp.maximum(asked_for.reshape(-1), 0)
    label_marks = labels.astype(jnp.bfloat16)
    payload_width = keyval_own.shape[-1]
    outgoing = (
        keyval_own[served].reshape(dev_count, per_peer, block_rows, payload_width),
        label_marks[served].reshape(dev_count, per_peer, block_rows),
    )
    fetched, fetched_marks = across_dev(outgoing)
    remote, remote_marks = across_region((keyval_own, label_marks), -1)
    fetched = fetched.reshape(slot_total, block_rows, payload_width)
    fetched_marks = fetched_marks.reshape(slot_total, block_rows)
    keyval_fetched = fetched
    slot_table = slot_number.reshape(block_count, 4)
    cross_index = neighbours[:, 5] % block_count
    d_attention = jnp.einsum(
        "re,de->rd", cotangent, w_out, preferred_element_type=jnp.float32
    ).astype(jnp.bfloat16)
    query_blocks = queries.reshape(block_count, block_rows, model_width)
    grad_blocks = d_attention.reshape(block_count, block_rows, model_width)
    query_marks = labels.astype(jnp.float32)

    def group_step(carried, group_index):
        own_back, inside_back, across_back = carried
        block_ids = group_index * group_size + jnp.arange(group_size, dtype=jnp.int32)
        middle_ids = slot_table[block_ids]
        far_ids = cross_index[block_ids]
        keyval = jnp.concatenate(
            [keyval_own[block_ids][:, None], keyval_fetched[middle_ids], remote[far_ids][:, None]],
            axis=1,
        )
        key_marks = jnp.concatenate(
            [
                label_marks[block_ids][:, None],
                fetched_marks[middle_ids],
                remote_marks[far_ids][:, None],
            ],
            axis=1,
        )
        key_marks = key_marks.astype(jnp.float32).reshape(group_size, -1)
        allowed = jnp.abs(query_marks[block_ids][:, :, None] - key_marks[:, None, :]) <= 1.0

        def local_attention(query_rows, key_pairs):
            return jax.vmap(attend)(query_rows, key_pairs, allowed)

        mixture, pullback = jax.vjp(local_attention, query_blocks[block_ids], keyval)
        d_query, d_pairs = pullback(grad_blocks[block_ids])
        own_back = own_back.at[block_ids].set(d_pairs[:, 0])
        inside_back = inside_back.at[middle_ids.reshape(-1)].set(
            d_pairs[:, 1:5].reshape(-1, block_rows, 2 * model_width)
        )
        across_back = across_back.at[far_ids].set(d_pairs[:, 5])
        return ((own_back, inside_back, across_back), (mixture, d_query))

    start = (
        jnp.zeros((block_count, block_rows, 2 * model_width), jnp.bfloat16),
        jnp.zeros((slot_total, block_rows, 2 * model_width), jnp.bfloat16),
        jnp.zeros((block_count, block_rows, 2 * model_width), jnp.bfloat16),
    )
    carried, (mixture, d_query) = lax.scan(
        group_step, start, jnp.arange(block_count // group_size, dtype=jnp.int32)
    )
    own_back, inside_back, across_back = carried
    attention = mixture.reshape(-1, model_width)
    branch_out = jnp.dot(attention, w_out, preferred_element_type=jnp.float32).astype(jnp.bfloat16)
    returned_pairs = across_dev(
        inside_back.reshape(dev_count, per_peer, block_rows, 2 * model_width)
    )
    across_pairs = across_region(across_back, 1)
    stacked_normed = jnp.concatenate([normed_blocks, normed_blocks[served], normed_blocks], axis=0)
    stacked_pairs = jnp.concatenate(
        [own_back, returned_pairs.reshape(slot_total, block_rows, 2 * model_width), across_pairs],
        axis=0,
    )
    grad_pairs, stacked_parts = pair_terms(stacked_normed, stacked_pairs, w_key, w_value)
    own_parts = stacked_parts[:block_count]
    returned = stacked_parts[block_count : block_count + slot_total]
    across_parts = stacked_parts[block_count + slot_total :]
    owner_hits = (
        asked_for.reshape(-1)[:, None] == jnp.arange(block_count, dtype=jnp.int32)[None, :]
    ).astype(jnp.bfloat16)
    inside_sum = jnp.einsum(
        "sb,sx->bx",
        owner_hits,
        returned.reshape(slot_total, -1),
        preferred_element_type=jnp.float32,
    )
    parts_total = (
        own_parts.astype(jnp.float32)
        + inside_sum.reshape(own_parts.shape)
        + across_parts.astype(jnp.float32)
    )
    d_queries = d_query.reshape(-1, model_width)
    grad_query = jnp.einsum("rd,re->de", normed, d_queries, preferred_element_type=jnp.float32)
    grad_output = jnp.einsum("rd,re->de", attention, cotangent, preferred_element_type=jnp.float32)
    d_normed = jnp.einsum("re,de->rd", d_queries, w_query, preferred_element_type=jnp.float32)
    d_normed = d_normed + parts_total.reshape(-1, model_width)
    grad_gain, grad_states = normalize_back(states, norm_gain, inverse, d_normed)
    summed = lax.psum(
        (
            grad_query,
            grad_pairs[:, :model_width],
            grad_pairs[:, model_width:],
            grad_output,
            grad_gain,
        ),
        ("region", "dev"),
    )
    grad_scale = 1.0 / math.sqrt(state_total)
    return (
        branch_out,
        grad_states,
        summed[0] * grad_scale,
        summed[1] * grad_scale,
        summed[2] * grad_scale,
        summed[3] * grad_scale,
        summed[4] * grad_scale,
    )


def solution(mesh):
    in_specs = (
        P(("region", "dev"), None),
        P(),
        P(),
        P(),
        P(),
        P(),
        P(("region", "dev"), None),
        P(("region", "dev"), None),
        P(("region", "dev"), None),
    )
    out_specs = (P(("region", "dev"), None), P(("region", "dev"), None), P(), P(), P(), P(), P())
    return jax.shard_map(body, mesh=mesh, in_specs=in_specs, out_specs=out_specs, check_vma=False)
```

profile of v0, /device:TPU:1, one launch (start us, length us, event | category | flops | bytes accessed | tf_op | source)
XLA Modules:
  0.0 490.1 jit_solution(7732689495440973424)
XLA Ops:
  9.1 8.6 %all-to-all-start = ((s32[32,1,1]{2,1,0:T(1,128)}), s32[32,1,1]{2,1,0:T(1,128)S(1)}, u32[]{:S(2)}, u32[]{:S(2)}) async-start(s32[32,1,1]{2,1,0:T(1,128)} %copy.110), calls=%async_computation | async-start | bytes 32768 | tf_op jit(solution)/shard_map/all_to_all | solution.py:123
  27.0 5.1 %all-to-all-start.2 = ((bf16[32,1,128]{2,1,0:T(2,128)(2,1)}), bf16[32,1,128]{2,1,0:T(2,128)(2,1)S(1)}, u32[]{:S(2)}, u32[]{:S(2)}) async-start(bf16[32,1,128]{2,1,0:T(2,128)(2,1)} %copy.112), calls=%async_computation.2 | async-start | bytes 32768 | tf_op jit(solution)/shard_map/all_to_all | solution.py:84
  32.2 4.8 gather_fusion.1
  39.0 5.6 %all-to-all-start.1 = ((bf16[32,1,128,1024]{3,2,1,0:T(8,128)(2,1)}), bf16[32,1,128,1024]{3,2,1,0:T(8,128)(2,1)}, u32[]{:S(2)}, u32[]{:S(2)}) async-start(bf16[32,1,128,1024]{3,2,1,0:T(8,128)(2,1)} %bitcast.133), calls=%async_computation.1 | async-start | bytes 16777216 | tf_op jit(solution)/shard_map/all_to_all | solution.py:84
  44.6 3.9 collective-permute-start.1
  63.9 80.4 %all-to-all-done.1 = bf16[32,1,128,1024]{3,2,1,0:T(8,128)(2,1)} async-done(((bf16[32,1,128,1024]{3,2,1,0:T(8,128)(2,1)}), bf16[32,1,128,1024]{3,2,1,0:T(8,128)(2,1)}, u32[]{:S(2)}, u32[]{:S(2)}) %all-to-all-start.1) | async-done | bytes 8388640 | tf_op jit(solution)/shard_map/all_to_all | solution.py:84
  144.3 4.1 gather_fusion.3
  154.7 3.8 fusion.19
  158.6 3.9 fusion.5
  175.1 4.3 broadcast_in_dim.107
  179.4 5.0 %scatter_fusion.1 = bf16[32,128,1024]{2,1,0:T(8,128)(2,1)} fusion(bf16[32,128,1024]{2,1,0:T(8,128)(2,1)} %broadcast_in_dim.107, s32[8]{0:T(128)S(1)} %fusion.56, bf16[8,128,1024]{2,1,0:T(8,128)(2,1)S(1)} %bitcast.139), kind=kCustom, calls=%fused_computation.15 | custom fusion | bytes 6291488 | tf_op jit(solution)/shard_map/while/body/eval_jaxpr/scatter | solution.py:173
  184.5 11.0 %all-to-all-start.3 = ((bf16[32,1,128,1024]{3,2,1,0:T(8,128)(2,1)}), bf16[32,1,128,1024]{3,2,1,0:T(8,128)(2,1)}, u32[]{:S(2)}, u32[]{:S(2)}) async-start(bf16[32,1,128,1024]{3,2,1,0:T(8,128)(2,1)} %bitcast.132), calls=%async_computation.3 | async-start | bytes 16777216 | tf_op jit(solution)/shard_map/all_to_all | solution.py:84
  199.2 6.5 %copy.127 = bf16[32,128,512]{1,2,0:T(8,128)(2,1)} copy(bf16[32,128,512]{2,1,0:T(8,128)(2,1)} %gather_fusion.13) | data formatting | bytes 8388608 | tf_op jit(solution)/shard_map/gather | solution.py:194
  205.8 5.3 %fusion.24 = bf16[2,128,8,64]{1,3,2,0:T(8,128)(2,1)S(1)} fusion(bf16[2,768,8,64]{1,3,2,0:T(8,128)(2,1)S(1)} %bitcast.149, bf16[2,8,128,768]{3,2,1,0:T(8,128)(2,1)} %copy-done.22, f32[2,8,128,768]{3,2,1,0:T(8,128)} %copy-done.21, f32[2,8,128]{2,1,0:T(8,128)S(1)} %neg.7, f32[2,8,128]{2,1,0:T(8,128)S(1)} %get-tuple-element.80, ...), kind=kOutput, calls=%fused_computation.58 | convolution fusion | flops 212467712 | bytes 11485184 | tf_op jit(solution)/shard_map/while/body/eval_jaxpr/transpose(jvp(vmap(qhd,khd->hqk)))/dot_general | solution.py:70
  223.3 7.8 %collective-permute-done.2 = bf16[2,128,1024]{2,1,0:T(8,128)(2,1)} collective-permute-done((bf16[2,128,1024]{2,1,0:T(8,128)(2,1)S(1)}, bf16[2,128,1024]{2,1,0:T(8,128)(2,1)}, u32[]{:S(2)}, u32[]{:S(2)}) %collective-permute-start.2) | collective-permute-done | bytes 524320 | tf_op jit(solution)/shard_map/ppermute | solution.py:21
  231.0 64.2 %all-to-all-done.3 = bf16[32,1,128,1024]{3,2,1,0:T(8,128)(2,1)} async-done(((bf16[32,1,128,1024]{3,2,1,0:T(8,128)(2,1)}), bf16[32,1,128,1024]{3,2,1,0:T(8,128)(2,1)}, u32[]{:S(2)}, u32[]{:S(2)}) %all-to-all-start.3) | async-done | bytes 8388640 | tf_op jit(solution)/shard_map/all_to_all | solution.py:84
  295.2 10.0 %fusion.20 = f32[512,1024]{1,0:T(8,128)S(1)} fusion(bf16[2,128,512]{1,2,0:T(8,128)(2,1)} %copy.126, bf16[32,128,512]{1,2,0:T(8,128)(2,1)} %copy.127, bf16[2,128,1024]{2,1,0:T(8,128)(2,1)} %collective-permute-done.2, bf16[32,128,1024]{2,1,0:T(8,128)(2,1)} %bitcast.34, bf16[2,128,1024]{2,1,0:T(8,128)(2,1)S(1)} %scatter_fusion), kind=kOutput, calls=%fused_computation.48 | convolution fusion | flops 4845993984 | bytes 15990784 | tf_op jit(solution)/shard_map/rd,re->de/dot_general | solution.py:48
  306.7 6.5 %pad_maximum_fusion = bf16[36,128,1024]{2,1,0:T(8,128)(2,1)S(1)} fusion(bf16[2,128,1024]{2,1,0:T(8,128)(2,1)} %collective-permute-done.2, bf16[32,128,1024]{2,1,0:T(8,128)(2,1)} %bitcast.34, bf16[2,128,1024]{2,1,0:T(8,128)(2,1)S(1)} %scatter_fusion), kind=kLoop, calls=%fused_computation.17 | loop fusion | flops 9437184 | bytes 18874368 | tf_op jit(solution)/shard_map/concatenate | solution.py:195
  313.2 5.8 %fusion.7 = f32[4608,512]{1,0:T(8,128)} fusion(bf16[512,512]{1,0:T(8,128)(2,1)S(1)} %copy-done, bf16[4608,1024]{1,0:T(8,128)(2,1)S(1)} %bitcast.130), kind=kOutput, calls=%fused_computation.30 | convolution fusion | flops 2415919104 | bytes 14680064 | tf_op jit(solution)/shard_map/re,de->rd/dot_general | solution.py:54
  319.6 6.7 %add_convert_fusion = bf16[4608,512]{1,0:T(8,128)(2,1)S(1)} fusion(f32[4608,512]{1,0:T(8,128)} %fusion.7, bf16[512,512]{1,0:T(8,128)(2,1)S(1)} %copy-done.8, bf16[4608,1024]{1,0:T(8,128)(2,1)} %bitcast.131), kind=kOutput, calls=%fused_computation.18 | convolution fusion | flops 2420637696 | bytes 19398656 | tf_op jit(solution)/shard_map/re,de->rd/dot_general | solution.py:51
  330.7 5.8 %reshape.377 = bf16[32,65536]{1,0:T(8,128)(2,1)} reshape(bf16[4096,512]{1,0:T(8,128)(2,1)} %slice.100) | data formatting | bytes 8388608 | tf_op jit(solution)/shard_map/reshape | solution.py:209
  341.2 70.4 %psum.39 = f32[512]{0:T(512)S(1)} all-reduce(f32[512]{0:T(512)S(1)} %get-tuple-element.41), channel_id=1, replica_groups=mesh['region'=4,'dev'=32] {'region','dev'}, use_global_device_ids=true, to_apply=%region_14.15 | all-reduce | flops 512 | bytes 4096 | tf_op jit(solution)/shard_map/psum | solution.py:223
  413.1 65.3 %all-reduce.5.cloned.1.call-done = (f32[512,512]{1,0:T(8,128)}, f32[512,512]{1,0:T(8,128)}, f32[512,512]{1,0:T(8,128)}, f32[512,512]{1,0:T(8,128)}) async-done(((f32[512,512]{1,0:T(8,128)}, f32[512,512]{1,0:T(8,128)}, f32[512,512]{1,0:T(8,128)}, f32[512,512]{1,0:T(8,128)}), (f32[512,512]{1,0:T(8,128)}, f32[512,512]{1,0:T(8,128)}, f32[512,512]{1,0:T(8,128)}, ...) | async-done | bytes 4194320 | tf_op jit(solution)/shard_map/psum | solution.py:223
  478.4 3.2 broadcast_multiply_fusion.2
  (142 shorter events, 77.5 us)
Async XLA Ops:
  7.2 12.7 %copy-start = (bf16[512,512]{1,0:T(8,128)(2,1)S(1)}, bf16[512,512]{1,0:T(8,128)(2,1)}, u32[]{:S(2)}) copy-start(bf16[512,512]{1,0:T(8,128)(2,1)} %param.13) | copy-start | bytes 1572868
  9.1 15.5 %all-to-all-start = ((s32[32,1,1]{2,1,0:T(1,128)}), s32[32,1,1]{2,1,0:T(1,128)S(1)}, u32[]{:S(2)}, u32[]{:S(2)}) async-start(s32[32,1,1]{2,1,0:T(1,128)} %copy.110), calls=%async_computation | async-start | bytes 32768 | tf_op jit(solution)/shard_map/all_to_all | solution.py:123
  27.0 12.0 %all-to-all-start.2 = ((bf16[32,1,128]{2,1,0:T(2,128)(2,1)}), bf16[32,1,128]{2,1,0:T(2,128)(2,1)S(1)}, u32[]{:S(2)}, u32[]{:S(2)}) async-start(bf16[32,1,128]{2,1,0:T(2,128)(2,1)} %copy.112), calls=%async_computation.2 | async-start | bytes 32768 | tf_op jit(solution)/shard_map/all_to_all | solution.py:84
  39.0 11.8 %copy-start.20 = (s32[2,6]{1,0:T(2,128)S(1)}, s32[2,6]{1,0:T(2,128)}, u32[]{:S(2)}) copy-start(s32[2,6]{1,0:T(2,128)} %param.15) | copy-start | bytes 148
  39.0 13.5 %copy-start.9 = (bf16[512,512]{1,0:T(8,128)(2,1)S(1)}, bf16[512,512]{1,0:T(8,128)(2,1)}, u32[]{:S(2)}) copy-start(bf16[512,512]{1,0:T(8,128)(2,1)} %param.11) | copy-start | bytes 1572868
  39.0 13.8 %copy-start.14 = (bf16[256,512]{1,0:T(8,128)(2,1)S(1)}, bf16[256,512]{1,0:T(8,128)(2,1)}, u32[]{:S(2)}) copy-start(bf16[256,512]{1,0:T(8,128)(2,1)} %param.17) | copy-start | bytes 786436
  39.0 13.8 %copy-start.15 = (bf16[512,512]{1,0:T(8,128)(2,1)S(1)}, bf16[512,512]{1,0:T(8,128)(2,1)}, u32[]{:S(2)}) copy-start(bf16[512,512]{1,0:T(8,128)(2,1)} %param.14) | copy-start | bytes 1572868
  39.0 105.3 %all-to-all-start.1 = ((bf16[32,1,128,1024]{3,2,1,0:T(8,128)(2,1)}), bf16[32,1,128,1024]{3,2,1,0:T(8,128)(2,1)}, u32[]{:S(2)}, u32[]{:S(2)}) async-start(bf16[32,1,128,1024]{3,2,1,0:T(8,128)(2,1)} %bitcast.133), calls=%async_computation.1 | async-start | bytes 16777216 | tf_op jit(solution)/shard_map/all_to_all | solution.py:84
  44.6 11.9 %collective-permute-start.1 = (bf16[2,128]{1,0:T(2,128)(2,1)S(1)}, bf16[2,128]{1,0:T(2,128)(2,1)S(1)}, u32[]{:S(2)}, u32[]{:S(2)}) collective-permute-start(bf16[2,128]{1,0:T(2,128)(2,1)S(1)} %get-tuple-element.77), channel_id=1, source_target_pairs={{0,96},{32,0},{64,32},{96,64},{1,97},{33,1},{65,33},{97,65},{2,98}... | collective-permute-start | bytes 1544 | tf_op jit(solution)/shard_map/ppermute | solution.py:21
  48.5 13.0 %collective-permute-start = (bf16[2,128,1024]{2,1,0:T(8,128)(2,1)S(1)}, bf16[2,128,1024]{2,1,0:T(8,128)(2,1)}, u32[]{:S(2)}, u32[]{:S(2)}) collective-permute-start(bf16[2,128,1024]{2,1,0:T(8,128)(2,1)S(1)} %bitcast.126), channel_id=1, source_target_pairs={{0,96},{32,0},{64,32},{96,64},{1,97},{33,1},{65,33},{97,65},{2,98}... | collective-permute-start | bytes 1572872 | tf_op jit(solution)/shard_map/ppermute | solution.py:21
  154.7 7.8 %copy-start.5 = (bf16[2,768,512]{1,2,0:T(8,128)(2,1)}, bf16[2,768,512]{1,2,0:T(8,128)(2,1)S(1)}, u32[]{:S(2)}) copy-start(bf16[2,768,512]{1,2,0:T(8,128)(2,1)S(1)} %copy.111) | copy-start | bytes 4718596
  154.7 3.9 copy-start.11
  158.6 4.0 copy-start.21
  184.5 110.8 %all-to-all-start.3 = ((bf16[32,1,128,1024]{3,2,1,0:T(8,128)(2,1)}), bf16[32,1,128,1024]{3,2,1,0:T(8,128)(2,1)}, u32[]{:S(2)}, u32[]{:S(2)}) async-start(bf16[32,1,128,1024]{3,2,1,0:T(8,128)(2,1)} %bitcast.132), calls=%async_computation.3 | async-start | bytes 16777216 | tf_op jit(solution)/shard_map/all_to_all | solution.py:84
  195.4 283.0 %all-reduce.5.cloned.1.call-start = ((), (), s32[]{:S(2)}) async-start(), calls=%async_computation.4 | async-start | bytes 8388608 | tf_op jit(solution)/shard_map/psum | solution.py:223
  199.2 6.5 %copy-start.10 = (bf16[2,768,512]{1,2,0:T(8,128)(2,1)S(1)}, bf16[2,768,512]{1,2,0:T(8,128)(2,1)}, u32[]{:S(2)}) copy-start(bf16[2,768,512]{1,2,0:T(8,128)(2,1)} %copy.116) | copy-start | bytes 4718596
  199.2 6.5 %copy-start.18 = (pred[2,128,768]{2,1,0:T(8,128)(4,1)S(1)}, pred[2,128,768]{2,1,0:T(8,128)(4,1)}, u32[]{:S(2)}) copy-start(pred[2,128,768]{2,1,0:T(8,128)(4,1)} %abs_compare_fusion) | copy-start | bytes 589828
  205.8 5.6 %copy-start.3 = (bf16[2,8,128,768]{3,2,1,0:T(8,128)(2,1)S(1)}, bf16[2,8,128,768]{3,2,1,0:T(8,128)(2,1)}, u32[]{:S(2)}) copy-start(bf16[2,8,128,768]{3,2,1,0:T(8,128)(2,1)} %get-tuple-element.50) | copy-start | bytes 9437188
  205.8 5.6 %copy-start.6 = (bf16[2,768,512]{1,2,0:T(8,128)(2,1)S(1)}, bf16[2,768,512]{1,2,0:T(8,128)(2,1)}, u32[]{:S(2)}) copy-start(bf16[2,768,512]{1,2,0:T(8,128)(2,1)} %copy-done.5) | copy-start | bytes 4718596
  214.9 16.1 %collective-permute-start.2 = (bf16[2,128,1024]{2,1,0:T(8,128)(2,1)S(1)}, bf16[2,128,1024]{2,1,0:T(8,128)(2,1)}, u32[]{:S(2)}, u32[]{:S(2)}) collective-permute-start(bf16[2,128,1024]{2,1,0:T(8,128)(2,1)S(1)} %scatter_fusion.2), channel_id=1, source_target_pairs={{0,32},{32,64},{64,96},{96,0},{1,33},{33,65},{65,97},{97,1},{2,34}... | collective-permute-start | bytes 1572872 | tf_op jit(solution)/shard_map/ppermute | solution.py:21
  313.2 6.4 %copy-start.1 = (bf16[36,128,1024]{2,1,0:T(8,128)(2,1)}, bf16[36,128,1024]{2,1,0:T(8,128)(2,1)S(1)}, u32[]{:S(2)}) copy-start(bf16[36,128,1024]{2,1,0:T(8,128)(2,1)S(1)} %pad_maximum_fusion) | copy-start | bytes 28311556
  313.2 6.4 %copy-start.8 = (bf16[512,512]{1,0:T(8,128)(2,1)S(1)}, bf16[512,512]{1,0:T(8,128)(2,1)}, u32[]{:S(2)}) copy-start(bf16[512,512]{1,0:T(8,128)(2,1)} %param.12) | copy-start | bytes 1572868
  336.6 4.1 copy-start.7
  336.6 4.1 copy-start.19
  (7 other events, 20.3 us)
Sparse Core Ops, SparseCore 0:
  319.8 158.5 all-reduce.4
where the time goes:
time: 491 us; the launch traced here: 490 us
  waiting for transfers between devices  225 us (46%)
  blocking collectives  70.4 us (14%)
  local copies, waits for them, and re-layouts  68.2 us (14%)
  matrix products  53.2 us (11%)
  starting transfers between devices  36.5 us (7%)
  other arithmetic  22.3 us (5%)
  between operations  14.6 us (3%)
    all_to_all x3, waiting for transfers between devices, across_dev(): lax.all_to_all(shortened(parcel), 'dev', split_axis=0, concat_axis=0, til...  147 us
    psum x1, blocking collectives, body(): lax.psum((grad_query, grad_pairs[:, :model_width], grad_pairs[:, model_wi...  70.4 us
    psum x1, waiting for transfers between devices, body(): lax.psum((grad_query, grad_pairs[:, :model_width], grad_pairs[:, model_wi...  65.3 us
    all_to_all x3, starting transfers between devices, across_dev(): lax.all_to_all(shortened(parcel), 'dev', split_axis=0, concat_axis=0, til...  21.7 us
    dot_general x3, matrix products, attend(): jnp.einsum('qhd,khd->hqk', query_heads, key_heads, preferred_element_type...  11.9 us
    ppermute x3, waiting for transfers between devices, passed_along(): return lax.ppermute(value, axis, pairs)  10.6 us
    dot_general x1, matrix products, pair_terms(): jnp.einsum('rd,re->de', flat_normed, flat_pairs, preferred_element_type=j...  10 us
  transfers between devices with their start and end apart: 8, of which 7 were waited for; matrix products, arithmetic and copies ran while one was open for 14% of the time, Pallas kernels for 0%

commit v1 on v0

v1 whole, which is shorter than its diff:
```python
import math

import jax
import jax.numpy as jnp
from jax import lax
from jax.experimental import pallas as pl
from jax.experimental.pallas import tpu as pltpu
from jax.sharding import PartitionSpec as P

MESH = pl.DeviceIdType.MESH
HEADS = 8
EPSILON = 1e-05
F32 = jnp.float32
BF16 = jnp.bfloat16
VMEM_LIMIT = 56 * 1024 * 1024
NN = (((1,), (0,)), ((), ()))
NT = (((1,), (1,)), ((), ()))
TN = (((0,), (0,)), ((), ()))


def dot(left, right, how=NN):
    return lax.dot_general(left, right, how, preferred_element_type=F32)


def place():
    r = lax.axis_index("region")
    d = lax.axis_index("dev")
    c = lax.rem(d, 2)
    x = lax.rem(lax.div(d, 2), 4)
    y = lax.div(d, 8)
    return r, c, x * (1 - c) + y * c, y * (1 - c) + x * c


def turn(value, step):
    return lax.rem(value + step + 4, 4)


def dev_at(a, b, c):
    return ((b * (1 - c) + a * c) * 4 + a * (1 - c) + b * c) * 2 + c


def around(value):
    return [value, turn(value, -1), turn(value, 1), turn(value, 2)]


def gather_kernel(states, labels, g, gl, far, fl, ssem, rsem, csend, crecv, lsem, lrsem, zsem, zrsem, own_sem):
    r, c, a, b = place()
    def to_dev(dev):
        return (r, dev)
    ap, am = to_dev(dev_at(turn(a, 1), b, c)), to_dev(dev_at(turn(a, -1), b, c))
    bp, bm = to_dev(dev_at(a, turn(b, 1), c)), to_dev(dev_at(a, turn(b, -1), c))
    mate = to_dev(lax.axis_index("dev") + 1 - 2 * c)
    zm, zp = (turn(r, -1), lax.axis_index("dev")), (turn(r, 1), lax.axis_index("dev"))
    barrier = pltpu.get_barrier_semaphore()
    for n in (ap, am, bp, bm, mate, zm, zp):
        pl.semaphore_signal(barrier, inc=1, device_id=n, device_id_type=MESH)
    pl.semaphore_wait(barrier, 7)
    started = []
    def send(src, dst, dev, s, q):
        copy = pltpu.make_async_remote_copy(src_ref=src, dst_ref=dst, send_sem=s, recv_sem=q, device_id=dev, device_id_type=MESH)
        copy.start()
        started.append(copy)
    def got(dst, s, q):
        pltpu.make_async_remote_copy(src_ref=dst, dst_ref=dst, send_sem=s, recv_sem=q, device_id=mate, device_id_type=MESH).wait_recv()
    lo, hi = pl.ds(0, 128), pl.ds(128, 128)
    ak = [a, turn(a, -1), turn(a, 1), turn(a, 2)]
    bk = [b, turn(b, -1), turn(b, 1), turn(b, 2)]
    def slot(i, j):
        return g.at[c, bk[j], ak[i]]
    def oslot(i, j):
        return g.at[1 - c, bk[j], ak[i]]
    def run(index, src, dst, dev):
        send(src, dst, dev, ssem.at[index], rsem.at[index])
    def arrived(index, dst):
        got(dst, ssem.at[index], rsem.at[index])
    def cross(i, j):
        src = states if i == 0 and j == 0 else slot(i, j)
        send(src, slot(i, j), mate, csend.at[i * 4 + j], crecv.at[i * 4 + j])
    run(0, states, slot(0, 0), ap)
    run(1, states, slot(0, 0), am)
    run(4, states, slot(0, 0), bp)
    run(5, states, slot(0, 0), bm)
    send(states, far, zm, zsem.at[0], zrsem.at[0])
    send(labels, fl, zm, zsem.at[1], zrsem.at[1])
    lrow = gl.at[c, b, a]
    send(labels, lrow, ap, lsem.at[0], lrsem.at[0])
    send(labels, lrow, am, lsem.at[1], lrsem.at[1])
    cross(0, 0)
    own = [pltpu.make_async_copy(states, slot(0, 0), own_sem.at[0]), pltpu.make_async_copy(labels, lrow, own_sem.at[1])]
    for o in own:
        o.start()
    got(gl.at[c, b, ak[1]], lsem.at[0], lrsem.at[0])
    send(gl.at[c, b, ak[1]], gl.at[c, b, ak[1]], ap, lsem.at[2], lrsem.at[2])
    got(gl.at[c, b, ak[2]], lsem.at[1], lrsem.at[1])
    arrived(0, slot(1, 0))
    run(2, slot(1, 0).at[lo], slot(1, 0).at[lo], ap)
    run(8, slot(1, 0), slot(1, 0), bp)
    run(9, slot(1, 0), slot(1, 0), bm)
    cross(1, 0)
    arrived(1, slot(2, 0))
    run(3, slot(2, 0).at[hi], slot(2, 0).at[hi], am)
    run(12, slot(2, 0), slot(2, 0), bp)
    run(13, slot(2, 0), slot(2, 0), bm)
    cross(2, 0)
    for o in own:
        o.wait()
    got(gl.at[c, b, ak[3]], lsem.at[2], lrsem.at[2])
    lline = gl.at[c, b]
    send(lline, lline, bp, lsem.at[3], lrsem.at[3])
    send(lline, lline, bm, lsem.at[4], lrsem.at[4])
    def second(i):
        base = 4 + 4 * i
        arrived(base, slot(i, 1))
        run(base + 2, slot(i, 1).at[lo], slot(i, 1).at[lo], bp)
        cross(i, 1)
        arrived(base + 1, slot(i, 2))
        run(base + 3, slot(i, 2).at[hi], slot(i, 2).at[hi], bm)
        cross(i, 2)
    second(0)
    arrived(2, slot(3, 0).at[lo])
    arrived(3, slot(3, 0).at[hi])
    run(16, slot(3, 0), slot(3, 0), bp)
    run(17, slot(3, 0), slot(3, 0), bm)
    cross(3, 0)
    got(gl.at[c, bk[1]], lsem.at[3], lrsem.at[3])
    send(gl.at[c, bk[1]], gl.at[c, bk[1]], bp, lsem.at[5], lrsem.at[5])
    got(gl.at[c, bk[2]], lsem.at[4], lrsem.at[4])
    second(1)
    second(2)
    second(3)
    got(gl.at[c, bk[3]], lsem.at[5], lrsem.at[5])
    send(gl.at[c], gl.at[c], mate, lsem.at[6], lrsem.at[6])
    for i in range(4):
        base = 4 + 4 * i
        arrived(base + 2, slot(i, 3).at[lo])
        arrived(base + 3, slot(i, 3).at[hi])
        cross(i, 3)
    for i in range(4):
        for j in range(4):
            pltpu.make_async_remote_copy(src_ref=states, dst_ref=g.at[1 - c, ak[j], bk[i]], send_sem=csend.at[i * 4 + j], recv_sem=crecv.at[i * 4 + j], device_id=mate, device_id_type=MESH).wait_recv()
    got(gl.at[1 - c], lsem.at[6], lrsem.at[6])
    got(far, zsem.at[0], zrsem.at[0])
    got(fl, zsem.at[1], zrsem.at[1])
    for s in started:
        s.wait_send()

def gather(states, labels):
    dma = pltpu.SemaphoreType.DMA
    return pl.pallas_call(
        gather_kernel,
        out_shape=(
            jax.ShapeDtypeStruct((2, 4, 4, 256, 512), jnp.bfloat16),
            jax.ShapeDtypeStruct((2, 4, 4, 2, 128), jnp.int32),
            jax.ShapeDtypeStruct((256, 512), jnp.bfloat16),
            jax.ShapeDtypeStruct((2, 128), jnp.int32),
        ),
        in_specs=[pl.BlockSpec(memory_space=pl.ANY)] * 2,
        out_specs=[pl.BlockSpec(memory_space=pl.ANY)] * 4,
        scratch_shapes=[dma((20,)), dma((20,)), dma((16,)), dma((16,)), dma((7,)), dma((7,)), dma((2,)), dma((2,)), dma((2,))],
        compiler_params=pltpu.CompilerParams(collective_id=0, has_side_effects=True),
    )(states, labels)


def normalize(rows, gain):
    wide = rows.astype(F32)
    inverse = lax.rsqrt(jnp.mean(wide * wide, axis=-1, keepdims=True) + EPSILON)
    return (wide * inverse * gain).astype(BF16)


def attend_kernel(
    near_ref, states, gain, wq, wk, wv, wo, labels, cot, g, gl, far, fl,
    branch, parts, far_parts, base_t, grads, table,
    fetched, normed, q_own, d_att, keys, normed_keys, values, key_marks, bias,
    q_wide, d_wide, scores, d_probs, probs, d_scores, att, dq, kv_grad, kv_sum, sems,
):
    copies = []
    for b in range(2):
        for e in range(4):
            n = near_ref[b, 1 + e]
            dev = lax.rem(lax.div(n, 2), 32)
            c = lax.rem(dev, 2)
            x = lax.rem(lax.div(dev, 2), 4)
            y = lax.div(dev, 8)
            slot = c * 16 + (y * (1 - c) + x * c) * 4 + x * (1 - c) + y * c
            local = lax.rem(n, 2)
            copy = pltpu.make_async_copy(
                g.at[slot, pl.ds(pl.multiple_of(local * 128, 128), 128)],
                fetched.at[b * 4 + e], sems.at[b * 4 + e])
            copy.start()
            copies.append(copy)
            key_marks[b, :, (1 + e) * 128 : (2 + e) * 128] = jnp.broadcast_to(gl[slot, pl.ds(local, 1)], (8, 128)).astype(F32)

    def clear(k, _):
        table[k] = 8
        return 0

    lax.fori_loop(0, 64, clear, 0)
    for b in range(2):
        for e in range(4):
            table[lax.rem(near_ref[b, 1 + e], 64)] = b * 4 + e
    parts[8] = jnp.zeros((512, 128), BF16)
    gain_row = gain[...]
    for b in range(2):
        rows = slice(b * 128, (b + 1) * 128)
        normed[rows] = normalize(states[rows], gain_row)
        q_own[rows] = (dot(normed[rows], wq[...]) .astype(BF16) * 0.125).astype(BF16)
        d_att[rows] = dot(cot[rows], wo[...], NT).astype(BF16)
        normed_keys[b, :128] = normed[rows]
        m = lax.rem(near_ref[b, 5], 2)
        normed_keys[b, 640:] = normalize(far[pl.ds(pl.multiple_of(m * 128, 128), 128)], gain_row)
        key_marks[b, :, :128] = jnp.broadcast_to(labels[b : b + 1], (8, 128)).astype(F32)
        key_marks[b, :, 640:] = jnp.broadcast_to(fl[pl.ds(m, 1)], (8, 128)).astype(F32)
    for b in range(2):
        for e in range(4):
            copies[b * 4 + e].wait()
            normed_keys[b, (1 + e) * 128 : (2 + e) * 128] = normalize(fetched[b * 4 + e], gain_row)

    def project(k, _):
        b, e = lax.div(k, 6), lax.rem(k, 6)
        rows = pl.ds(pl.multiple_of(e * 128, 128), 128)
        n = normed_keys[b, rows]
        keys[b, rows] = dot(n, wk[...]).astype(BF16)
        values[b, rows] = dot(n, wv[...]).astype(BF16)
        return 0

    lax.fori_loop(0, 12, project, 0)
    head_of = lax.broadcasted_iota(jnp.int32, (128, 256), 1) // 64
    for b in range(2):
        rows = slice(b * 128, (b + 1) * 128)
        own = jnp.broadcast_to(labels[b : b + 1], (128, 128)).astype(F32).T
        for e in range(6):
            at = slice(e * 128, (e + 1) * 128)
            gap = jnp.abs(own - jnp.broadcast_to(key_marks[b, :1, at], (128, 128)))
            bias[:, at] = jnp.where(gap <= 1.0, 0.0, -jnp.inf)
        for half in range(2):
            cols = slice(half * 256, (half + 1) * 256)
            for i in range(4):
                at = slice(i * 128, (i + 1) * 128)
                q_wide[at] = jnp.where(head_of == i, q_own[rows, cols].astype(F32), 0.0).astype(BF16)
                d_wide[at] = jnp.where(head_of == i, d_att[rows, cols].astype(F32), 0.0).astype(BF16)
            scores[...] = dot(q_wide[...], keys[b, :, cols], NT)
            d_probs[...] = dot(d_wide[...], values[b, :, cols], NT)

            def soft(k, _):
                at = pl.ds(pl.multiple_of(k * 32, 32), 32)
                bt = pl.ds(pl.multiple_of(lax.rem(k, 4) * 32, 32), 32)
                w = jnp.exp(scores[at] + bias[bt])
                p = w * (1.0 / jnp.sum(w, axis=-1, keepdims=True))
                dp = d_probs[at]
                mean = jnp.sum(p * dp, axis=-1, keepdims=True)
                probs[at] = p.astype(BF16)
                d_scores[at] = (p * (dp - mean)).astype(BF16)
                return 0

            lax.fori_loop(0, 16, soft, 0)
            mixed = dot(probs[...], values[b, :, cols])
            turned = dot(d_scores[...], keys[b, :, cols])
            one = jnp.zeros((128, 256), F32)
            two = jnp.zeros((128, 256), F32)
            for i in range(4):
                at = slice(i * 128, (i + 1) * 128)
                one = one + jnp.where(head_of == i, mixed[at], 0.0)
                two = two + jnp.where(head_of == i, turned[at], 0.0)
            att[rows, cols] = one.astype(BF16)
            dq[rows, cols] = (two * 0.125).astype(BF16)
            kv_grad[b, cols] = dot(q_wide[...], d_scores[...], TN).astype(BF16)
            kv_grad[b, 512 + half * 256 : 768 + half * 256] = dot(d_wide[...], probs[...], TN).astype(BF16)
    branch[...] = dot(att[...], wo[...]).astype(BF16)
    grads[:512] = dot(normed[...], dq[...], TN).astype(BF16)
    grads[1536:] = dot(att[...], cot[...], TN).astype(BF16)
    mine = dot(wq[...], dq[...], NT)
    for b in range(2):
        for e in range(6):
            at = slice(e * 128, (e + 1) * 128)
            part = (dot(wk[...], kv_grad[b, :512, at]) + dot(wv[...], kv_grad[b, 512:, at])).astype(BF16)
            if e == 0:
                base_t[:, b * 128 : (b + 1) * 128] = mine[:, b * 128 : (b + 1) * 128] + part.astype(F32)
            elif e < 5:
                parts[b * 4 + e - 1] = part
            else:
                far_parts[lax.rem(near_ref[b, 5], 2)] = part
    for half in range(2):
        at = slice(half * 512, (half + 1) * 512)
        kv_sum[at] = dot(kv_grad[0, at], normed_keys[0]) + dot(kv_grad[1, at], normed_keys[1])
        grads[512 + half * 512 : 1024 + half * 512] = kv_sum[at].T.astype(BF16)


def attend(neighbours, states, gain, wq, wk, wv, wo, labels, cot, g, gl, far, fl):
    vmem = pl.BlockSpec(memory_space=pltpu.VMEM)
    smem = pl.BlockSpec(memory_space=pltpu.SMEM)
    anywhere = pl.BlockSpec(memory_space=pl.ANY)
    return pl.pallas_call(
        attend_kernel,
        out_shape=(
            jax.ShapeDtypeStruct((256, 512), BF16),
            jax.ShapeDtypeStruct((9, 512, 128), BF16),
            jax.ShapeDtypeStruct((2, 512, 128), BF16),
            jax.ShapeDtypeStruct((512, 256), F32),
            jax.ShapeDtypeStruct((2048, 512), BF16),
            jax.ShapeDtypeStruct((64,), jnp.int32),
        ),
        in_specs=[smem] + [vmem] * 8 + [anywhere] + [vmem] * 3,
        out_specs=[vmem] * 5 + [smem],
        scratch_shapes=[
            pltpu.VMEM((8, 128, 512), BF16),
            pltpu.VMEM((256, 512), BF16),
            pltpu.VMEM((256, 512), BF16),
            pltpu.VMEM((256, 512), BF16),
            pltpu.VMEM((2, 768, 512), BF16),
            pltpu.VMEM((2, 768, 512), BF16),
            pltpu.VMEM((2, 768, 512), BF16),
            pltpu.VMEM((2, 8, 768), F32),
            pltpu.VMEM((128, 768), F32),
            pltpu.VMEM((512, 256), BF16),
            pltpu.VMEM((512, 256), BF16),
            pltpu.VMEM((512, 768), F32),
            pltpu.VMEM((512, 768), F32),
            pltpu.VMEM((512, 768), BF16),
            pltpu.VMEM((512, 768), BF16),
            pltpu.VMEM((256, 512), BF16),
            pltpu.VMEM((256, 512), BF16),
            pltpu.VMEM((2, 1024, 768), BF16),
            pltpu.VMEM((1024, 512), F32),
            pltpu.SemaphoreType.DMA((8,)),
        ],
        compiler_params=pltpu.CompilerParams(vmem_limit_bytes=VMEM_LIMIT),
    )(neighbours, states, gain, wq, wk, wv, wo, labels, cot, g, gl, far, fl)


def scatter_kernel(
    table, parts, far_parts, base_t, grads, states, gain,
    grad_states, summed,
    give, take, far_send, far_recv, near_send, near_recv, line,
    far2_recv, near2_send, near2_recv, z_part, total,
    g_mate, g_half, gz_far, gz_near_send, gz_near, gy_own, gy_recv, gx_own, gx_recv,
    give_s, take_s, s1s, s1r, s2s, s2r, zs, zr, gs, gr,
):
    r, c, a, b = place()
    d = lax.axis_index("dev")
    x, y = lax.rem(lax.div(d, 2), 4), lax.div(d, 8)
    ak, bk = around(a), around(b)
    xk, yk, rk = around(x), around(y), around(r)
    mate = (r, d + 1 - 2 * c)
    a_to = [(r, dev_at(k, b, c)) for k in ak]
    b_to = [(r, dev_at(a, k, c)) for k in bk]
    x_to = [(r, (y * 4 + k) * 2 + c) for k in xk]
    y_to = [(r, (k * 4 + x) * 2 + c) for k in yk]
    z_to = [(k, d) for k in rk]
    barrier = pltpu.get_barrier_semaphore()
    peers = [mate] + x_to[1:] + y_to[1:] + z_to[1:3]
    for peer in peers:
        pl.semaphore_signal(barrier, inc=1, device_id=peer, device_id_type=MESH)
    pl.semaphore_wait(barrier, len(peers))
    started = []

    def send(src, dst, s, q, to):
        copy = pltpu.make_async_remote_copy(
            src_ref=src, dst_ref=dst, send_sem=s, recv_sem=q, device_id=to, device_id_type=MESH)
        copy.start()
        started.append(copy)

    def got(dst, s, q):
        pltpu.make_async_remote_copy(
            src_ref=dst, dst_ref=dst, send_sem=s, recv_sem=q, device_id=mate, device_id_type=MESH).wait_recv()

    mate_rows = pl.ds(pl.multiple_of((1 - c) * 1024, 1024), 1024)
    send(grads.at[mate_rows], g_mate, gs.at[0], gr.at[0], mate)
    send(far_parts, z_part, zs.at[0], zr.at[0], z_to[2])

    def fill(dev, into):
        for block in range(2):
            into[block] = parts[table[2 * dev + block]]

    order = (3, 1, 2, 0)
    for j in (3, 1, 2, 0):
        for i in order:
            k = i * 4 + j
            fill(dev_at(bk[i], ak[j], 1 - c), give.at[k])
            send(give.at[k], take.at[k], give_s.at[k], take_s.at[k], mate)

    def here(i, j, block, rows):
        k = i * 4 + j
        mine = parts[table[2 * dev_at(ak[i], bk[j], c) + block], rows]
        return mine.astype(F32) + take[k, block, rows].astype(F32)

    def each(body):
        def step(t, _):
            body(pl.ds(pl.multiple_of(t * 128, 128), 128))
            return 0

        lax.fori_loop(0, 4, step, 0)

    def took(i, j):
        got(take.at[i * 4 + j], give_s.at[i * 4 + j], take_s.at[i * 4 + j])

    got(g_mate, gs.at[0], gr.at[0])
    base = c * 1024

    def half_sum(t, _):
        rows = pl.ds(pl.multiple_of(t * 64, 64), 64)
        from_rows = pl.ds(pl.multiple_of(base + t * 64, 64), 64)
        g_half[rows] = (grads[from_rows].astype(F32) + g_mate[rows].astype(F32)).astype(BF16)
        return 0

    lax.fori_loop(0, 16, half_sum, 0)

    def z_rows(k, offset, size):
        return pl.ds(pl.multiple_of(rk[k] * 256 + offset, 16), size)

    send(g_half.at[z_rows(3, 0, 128)], gz_far.at[0], gs.at[1], gr.at[1], z_to[2])
    send(g_half.at[z_rows(3, 128, 128)], gz_far.at[1], gs.at[2], gr.at[2], z_to[1])

    for i in order:
        took(i, 3)
        for block in range(2):
            def far_sum(rows, block=block, i=i):
                far_send[i, block, rows] = here(i, 3, block, rows).astype(BF16)
            each(far_sum)
            send(far_send.at[i, block], far_recv.at[i, block], s1s.at[i * 4 + block], s1r.at[i * 4 + block], b_to[2 - block])

    for way in range(2):
        k = 2 - way
        got(gz_far.at[way], gs.at[1 + way], gr.at[1 + way])

        def z_near(t, _, way=way, k=k):
            rows = pl.ds(pl.multiple_of(t * 64, 64), 64)
            gz_near_send[way, rows] = g_half[z_rows(k, t * 64, 64)]
            return 0

        lax.fori_loop(0, 4, z_near, 0)
        both = slice(way * 128, way * 128 + 128)
        gz_near_send[way, both] = (gz_near_send[way, both].astype(F32) + gz_far[way].astype(F32)).astype(BF16)
        send(gz_near_send.at[way], gz_near.at[way], gs.at[3 + way], gr.at[3 + way], z_to[k])

    for i in order:
        for way in range(2):
            j = 2 - way
            took(i, j)
            got(far_recv.at[i, way], s1s.at[i * 4 + way], s1r.at[i * 4 + way])

            def near_sum(rows, way=way, i=i, j=j):
                near_send[i, way, way, rows] = (here(i, j, way, rows) + far_recv[i, way, rows].astype(F32)).astype(BF16)
                near_send[i, way, 1 - way, rows] = here(i, j, 1 - way, rows).astype(BF16)
            each(near_sum)
            send(near_send.at[i, way], near_recv.at[i, way], s1s.at[i * 4 + 2 + way], s1r.at[i * 4 + 2 + way], b_to[j])

    for way in range(2):
        got(gz_near.at[way], gs.at[3 + way], gr.at[3 + way])
    gy_own[...] = (g_half[z_rows(0, 0, 256)].astype(F32) + gz_near[0].astype(F32) + gz_near[1].astype(F32)).astype(BF16)

    def small(k, size, pos):
        return pl.ds(pl.multiple_of(pos[k] * size, 16), size)

    for k in range(1, 4):
        send(gy_own.at[small(k, 64, yk)], gy_recv.at[k - 1], gs.at[4 + k], gr.at[4 + k], y_to[k])

    def ring_end(i):
        took(i, 0)
        for way in range(2):
            got(near_recv.at[i, way], s1s.at[i * 4 + 2 + way], s1r.at[i * 4 + 2 + way])
        for block in range(2):
            def end(rows, block=block):
                line[i, block, rows] = (
                    here(i, 0, block, rows) + near_recv[i, 0, block, rows].astype(F32)
                    + near_recv[i, 1, block, rows].astype(F32)).astype(BF16)
            each(end)

    ring_end(3)
    for block in range(2):
        send(line.at[3, block], far2_recv.at[block], s2s.at[block], s2r.at[block], a_to[2 - block])
    ring_end(1)

    for k in range(1, 4):
        got(gy_recv.at[k - 1], gs.at[4 + k], gr.at[4 + k])
    gx_own[...] = (gy_own[small(0, 64, yk)].astype(F32) + gy_recv[0].astype(F32) + gy_recv[1].astype(F32) + gy_recv[2].astype(F32)).astype(BF16)
    for k in range(1, 4):
        send(gx_own.at[small(k, 16, xk)], gx_recv.at[k - 1], gs.at[7 + k], gr.at[7 + k], x_to[k])

    ring_end(2)
    for way in range(2):
        got(far2_recv.at[way], s2s.at[way], s2r.at[way])

        def near2(rows, way=way):
            near2_send[way, way, rows] = (line[2 - way, way, rows].astype(F32) + far2_recv[way, rows].astype(F32)).astype(BF16)
            near2_send[way, 1 - way, rows] = line[2 - way, 1 - way, rows]
        each(near2)
        send(near2_send.at[way], near2_recv.at[way], s2s.at[2 + way], s2r.at[2 + way], a_to[2 - way])

    for k in range(1, 4):
        got(gx_recv.at[k - 1], gs.at[7 + k], gr.at[7 + k])
    start = c * 1024 + r * 256 + y * 64 + x * 16

    def span(first, size):
        return pl.ds(pl.multiple_of(first, 16), size)

    summed[span(start, 16)] = (
        gx_own[small(0, 16, xk)].astype(F32) + gx_recv[0].astype(F32) + gx_recv[1].astype(F32) + gx_recv[2].astype(F32)).astype(BF16)

    def spread(pos, size, first, sem, to):
        for k in range(1, 4):
            send(summed.at[span(first + pos[0] * size, size)], summed.at[span(first + pos[0] * size, size)], gs.at[sem + k], gr.at[sem + k], to[k])

    def spread_in(pos, size, first, sem):
        for k in range(1, 4):
            source = pos[{1: 2, 2: 1, 3: 3}[k]]
            got(summed.at[span(first + source * size, size)], gs.at[sem + k], gr.at[sem + k])

    first_x = c * 1024 + r * 256 + y * 64
    spread(xk, 16, first_x, 10, x_to)
    ring_end(0)
    spread_in(xk, 16, first_x, 10)
    first_y = c * 1024 + r * 256
    spread(yk, 64, first_y, 13, y_to)
    spread_in(yk, 64, first_y, 13)
    first_z = c * 1024
    mine = summed.at[span(first_z + r * 256, 256)]
    send(mine, mine, gs.at[17], gr.at[17], z_to[1])
    send(mine, mine, gs.at[18], gr.at[18], z_to[2])

    for way in range(2):
        got(near2_recv.at[way], s2s.at[2 + way], s2r.at[2 + way])
    got(z_part, zs.at[0], zr.at[0])
    for block in range(2):
        def last(rows, block=block):
            at = slice(block * 128, block * 128 + 128)
            total[rows, at] = (
                base_t[rows, at] + line[0, block, rows].astype(F32) + near2_recv[0, block, rows].astype(F32)
                + near2_recv[1, block, rows].astype(F32) + z_part[block, rows].astype(F32))
        each(last)

    up, down = rk[1], rk[2]
    came_down = summed.at[span(first_z + down * 256, 256)]
    got(came_down, gs.at[17], gr.at[17])
    one = summed.at[span(first_z + down * 256, 128)]
    send(one, one, gs.at[19], gr.at[19], z_to[1])
    came_up = summed.at[span(first_z + up * 256, 256)]
    got(came_up, gs.at[18], gr.at[18])
    two = summed.at[span(first_z + up * 256 + 128, 128)]
    send(two, two, gs.at[20], gr.at[20], z_to[2])

    def finish(t, _):
        rows = pl.ds(pl.multiple_of(t * 128, 128), 128)
        d_normed = total[:, rows].T
        wide = states[rows].astype(F32)
        inverse = lax.rsqrt(jnp.mean(wide * wide, axis=-1, keepdims=True) + EPSILON)
        scaled = d_normed * gain[...]
        along = jnp.sum(scaled * wide, axis=-1, keepdims=True) * (1.0 / 512)
        grad_states[rows] = (inverse * scaled - wide * (inverse * inverse * inverse * along)).astype(BF16)
        return 0

    lax.fori_loop(0, 2, finish, 0)
    got(summed.at[span(first_z + rk[3] * 256, 128)], gs.at[19], gr.at[19])
    got(summed.at[span(first_z + rk[3] * 256 + 128, 128)], gs.at[20], gr.at[20])
    half = summed.at[span(first_z, 1024)]
    send(half, half, gs.at[21], gr.at[21], mate)
    got(summed.at[span(1024 - first_z, 1024)], gs.at[21], gr.at[21])
    for copy in started:
        copy.wait_send()


def scatter(table, parts, far_parts, base_t, grads, states, gain):
    vmem = pl.BlockSpec(memory_space=pltpu.VMEM)
    smem = pl.BlockSpec(memory_space=pltpu.SMEM)
    dma = pltpu.SemaphoreType.DMA
    return pl.pallas_call(
        scatter_kernel,
        out_shape=(jax.ShapeDtypeStruct((256, 512), BF16), jax.ShapeDtypeStruct((2048, 512), BF16)),
        in_specs=[smem] + [vmem] * 6,
        out_specs=[vmem] * 2,
        scratch_shapes=[
            pltpu.VMEM((16, 2, 512, 128), BF16),
            pltpu.VMEM((16, 2, 512, 128), BF16),
            pltpu.VMEM((4, 2, 512, 128), BF16),
            pltpu.VMEM((4, 2, 512, 128), BF16),
            pltpu.VMEM((4, 2, 2, 512, 128), BF16),
            pltpu.VMEM((4, 2, 2, 512, 128), BF16),
            pltpu.VMEM((4, 2, 512, 128), BF16),
            pltpu.VMEM((2, 512, 128), BF16),
            pltpu.VMEM((2, 2, 512, 128), BF16),
            pltpu.VMEM((2, 2, 512, 128), BF16),
            pltpu.VMEM((2, 512, 128), BF16),
            pltpu.VMEM((512, 256), F32),
            pltpu.VMEM((1024, 512), BF16),
            pltpu.VMEM((1024, 512), BF16),
            pltpu.VMEM((2, 128, 512), BF16),
            pltpu.VMEM((2, 256, 512), BF16),
            pltpu.VMEM((2, 256, 512), BF16),
            pltpu.VMEM((256, 512), BF16),
            pltpu.VMEM((3, 64, 512), BF16),
            pltpu.VMEM((64, 512), BF16),
            pltpu.VMEM((3, 16, 512), BF16),
            dma((16,)), dma((16,)), dma((16,)), dma((16,)), dma((4,)), dma((4,)), dma((1,)), dma((1,)),
            dma((22,)), dma((22,)),
        ],
        compiler_params=pltpu.CompilerParams(collective_id=1, has_side_effects=True, vmem_limit_bytes=VMEM_LIMIT),
    )(table, parts, far_parts, base_t, grads, states, gain)


def body(states, norm_gain, w_query, w_key, w_value, w_out, neighbours, labels, cotangent):
    gain = norm_gain.reshape(1, -1)
    g, gl, far, fl = gather(states, labels)
    branch_out, parts, far_parts, base_t, grads, table = attend(
        neighbours, states, gain, w_query, w_key, w_value, w_out, labels, cotangent,
        g.reshape(32, 256, 512), gl.reshape(32, 2, 128), far, fl)
    grad_states, summed = scatter(table, parts, far_parts, base_t, grads, states, gain)
    scale = 1.0 / math.sqrt(32768)
    full = summed.astype(F32).reshape(4, 512, 512) * scale
    along = (
        full[0] * w_query.astype(F32) + full[1] * w_key.astype(F32) + full[2] * w_value.astype(F32))
    grad_gain = jnp.sum(along, axis=1) / norm_gain
    return branch_out, grad_states, full[0], full[1], full[2], full[3], grad_gain


def solution(mesh):
    rows = P(("region", "dev"), None)
    return jax.shard_map(
        body, mesh=mesh,
        in_specs=(rows, P(), P(), P(), P(), P(), rows, rows, rows),
        out_specs=(rows, rows, P(), P(), P(), P(), P()),
        check_vma=False)
```

time: 491 us -> 141 us (0.29)
  waiting for transfers between devices: 225 us -> 0 us
  Pallas kernels: 0 us -> 134 us
  blocking collectives: 70.4 us -> 0 us
  local copies, waits for them, and re-layouts: 68.2 us -> 0.73 us
  matrix products: 53.2 us -> 0 us
  starting transfers between devices: 36.5 us -> 0 us
  other arithmetic: 22.3 us -> 5.29 us
  between operations: 14.6 us -> 0.73 us
    all_to_all x4 -> x0, waiting for transfers between devices: 149 us -> none  [the longest x3 147 us: across_dev(): lax.all_to_all(shortened(parcel), 'dev', split_axis=0, concat_axis=0, til...]
    pallas_call x0 -> x3, Pallas kernels: none -> 134 us  [the longest x1 64.8 us: scatter(): pl.pallas_call(scatter_kernel, out_shape=(jax.ShapeDtypeStruct((256, 512)...]
    psum x1 -> x0, blocking collectives: 70.4 us -> none  [body(): lax.psum((grad_query, grad_pairs[:, :model_width], grad_pairs[:, model_wi...]
    psum x1 -> x0, waiting for transfers between devices: 65.3 us -> none  [body(): lax.psum((grad_query, grad_pairs[:, :model_width], grad_pairs[:, model_wi...]
    dot_general x18 -> x0, matrix products: 53.2 us -> none  [the longest x3 11.9 us: attend(): jnp.einsum('qhd,khd->hqk', query_heads, key_heads, preferred_element_type...]
    all_to_all x4 -> x0, starting transfers between devices: 30.3 us -> none  [the longest x3 21.7 us: across_dev(): lax.all_to_all(shortened(parcel), 'dev', split_axis=0, concat_axis=0, til...]
    gather x17 -> x0, local copies, waits for them, and re-layouts: 28.9 us -> none  [the longest x2 9.42 us: body(): normed_blocks[served]]
    slice x9 -> x0, local copies, waits for them, and re-layouts: 10.8 us -> none  [the longest x2 2.99 us: attend(): key_heads = key_pairs[:, :model_width].reshape(key_count, HEADS, head_dim)]
  transfers between devices with their start and end apart: 8 -> 0, of which waited for: 7 -> 0; matrix products, arithmetic and copies ran while one was open for 14% -> 0% of each run, Pallas kernels for 0% -> 0%
where the time goes in v1:
time: 141 us
  Pallas kernels  134 us (95%)
  other arithmetic  5.29 us (4%)
    pallas_call x1, Pallas kernels, scatter(): pl.pallas_call(scatter_kernel, out_shape=(jax.ShapeDtypeStruct((256, 512)...  64.8 us
    pallas_call x1, Pallas kernels, gather(): pl.pallas_call(gather_kernel, out_shape=(jax.ShapeDtypeStruct((2, 4, 4, 2...  36.1 us
    pallas_call x1, Pallas kernels, attend(): pl.pallas_call(attend_kernel, out_shape=(jax.ShapeDtypeStruct((256, 512),...  33.3 us

profile of v1, /device:TPU:1, one launch (start us, length us, event | category | flops | bytes accessed | tf_op | source)
XLA Modules:
  0.0 140.9 jit_solution(3742722602115579415)
XLA Ops:
  0.6 36.1 %shard_map.144 = (bf16[2,4,4,256,512]{4,3,2,1,0:T(8,128)(2,1)}, s32[2,4,4,2,128]{4,3,2,1,0:T(2,128)}, bf16[256,512]{1,0:T(8,128)(2,1)}, s32[2,128]{1,0:T(2,128)}) custom-call(bf16[256,512]{1,0:T(8,128)(2,1)} %states.5, s32[2,128]{1,0:T(2,128)} %labels.3), custom_call_target="tpu_custom_call" | custom-call | tf_op jit(solution)/shard_map/pallas_call | solution.py:149
  36.7 33.3 %shard_map.145 = (bf16[256,512]{1,0:T(8,128)(2,1)}, bf16[9,512,128]{2,1,0:T(8,128)(2,1)}, bf16[2,512,128]{2,1,0:T(8,128)(2,1)}, f32[512,256]{1,0:T(8,128)}, bf16[2048,512]{1,0:T(8,128)(2,1)}, /*index=5*/s32[64]{0:T(128)}) custom-call(s32[2,6]{1,0:T(2,128)} %near_ref.1, bf16[256,512]{1,0:T(8,128)(2,1)} %states.5, f32[1,512]{1,0:T(1,128)} %bitcast.5, ...), custom_call_target="tpu_custom_call" | custom-call | tf_op jit(solution)/shard_map/pallas_call | solution.py:292
  70.0 64.8 %shard_map.146 = (bf16[256,512]{1,0:T(8,128)(2,1)}, bf16[2048,512]{1,0:T(8,128)(2,1)}) custom-call(s32[64]{0:T(128)} %get-tuple-element.24.table, bf16[9,512,128]{2,1,0:T(8,128)(2,1)} %get-tuple-element.25.parts, bf16[2,512,128]{2,1,0:T(8,128)(2,1)} %get-tuple-element.26.far_parts, f32[512,256]{1,0:T(8,128)} %get-tuple-element.27.base_t, ...), custom_call_target="tpu_custom_call" | custom-call | tf_op jit(solution)/shard_map/pallas_call | solution.py:565
  134.8 0.0 copy-start
  134.8 0.0 copy-start.1
  134.8 0.0 copy-start.2
  134.8 2.3 %convert_multiply_fusion = f32[2048,512]{1,0:T(8,128)S(1)} fusion(bf16[2048,512]{1,0:T(8,128)(2,1)} %get-tuple-element.30), kind=kLoop, calls=%fused_computation | loop fusion | flops 2097152 | bytes 6291456 | tf_op jit(solution)/shard_map/mul | solution.py:607
  137.1 0.0 copy-done
  137.1 0.0 copy-done.1
  137.1 0.0 copy-done.2
  137.2 0.0 copy-start.4
  137.2 0.0 copy-start.3
  137.2 2.4 %add_reduce_fusion = (f32[512]{0:T(512)S(1)}, f32[512,512]{1,0:T(8,128)}, f32[512,512]{1,0:T(8,128)}, f32[512,512]{1,0:T(8,128)}, f32[512,512]{1,0:T(8,128)}) fusion(bf16[512,512]{1,0:T(8,128)(2,1)S(1)} %copy-done.2, bf16[512,512]{1,0:T(8,128)(2,1)S(1)} %copy-done.1, bf16[512,512]{1,0:T(8,128)(2,1)S(1)} %copy-done, f32[2048,512]{1,0:T(8,128)S(1)} %convert_multiply_fusion), kind=kLoop, calls=%fused_computation.1 | loop fusion | flops 2358784 | bytes 9963520 | tf_op jit(solution)/shard_map/reduce_sum | solution.py:610
  139.6 0.0 copy-done.4
  139.6 0.6 div.3
  140.2 0.0 copy-done.3
  140.2 0.7 copy.17
Async XLA Ops:
  134.8 2.3 %copy-start = (bf16[512,512]{1,0:T(8,128)(2,1)S(1)}, bf16[512,512]{1,0:T(8,128)(2,1)}, u32[]{:S(2)}) copy-start(bf16[512,512]{1,0:T(8,128)(2,1)} %wq.1) | copy-start | bytes 1572868
  134.8 2.3 %copy-start.1 = (bf16[512,512]{1,0:T(8,128)(2,1)S(1)}, bf16[512,512]{1,0:T(8,128)(2,1)}, u32[]{:S(2)}) copy-start(bf16[512,512]{1,0:T(8,128)(2,1)} %wk.1) | copy-start | bytes 1572868
  134.8 2.3 %copy-start.2 = (bf16[512,512]{1,0:T(8,128)(2,1)S(1)}, bf16[512,512]{1,0:T(8,128)(2,1)}, u32[]{:S(2)}) copy-start(bf16[512,512]{1,0:T(8,128)(2,1)} %wv.1) | copy-start | bytes 1572868
  137.2 2.4 %copy-start.4 = (f32[512]{0:T(512)S(1)}, f32[512]{0:T(512)}, u32[]{:S(2)}) copy-start(f32[512]{0:T(512)} %param.10) | copy-start | bytes 6148
  137.2 3.0 %copy-start.3 = (bf16[256,512]{1,0:T(8,128)(2,1)S(1)}, bf16[256,512]{1,0:T(8,128)(2,1)}, u32[]{:S(2)}) copy-start(bf16[256,512]{1,0:T(8,128)(2,1)} %get-tuple-element.44) | copy-start | bytes 786436

commit v2 on v0

v2 whole, which is shorter than its diff:
```python
import math

import jax
import jax.numpy as jnp
from jax import lax
from jax.experimental import pallas as pl
from jax.experimental.pallas import tpu as pltpu
from jax.sharding import PartitionSpec as P

MESH = pl.DeviceIdType.MESH
HEADS = 8
EPSILON = 1e-05
F32 = jnp.float32
BF16 = jnp.bfloat16
VMEM_LIMIT = 56 * 1024 * 1024
NN = (((1,), (0,)), ((), ()))
NT = (((1,), (1,)), ((), ()))
TN = (((0,), (0,)), ((), ()))


def dot(left, right, how=NN):
    return lax.dot_general(left, right, how, preferred_element_type=F32)


def place():
    r = lax.axis_index("region")
    d = lax.axis_index("dev")
    c = lax.rem(d, 2)
    x = lax.rem(lax.div(d, 2), 4)
    y = lax.div(d, 8)
    return r, c, x * (1 - c) + y * c, y * (1 - c) + x * c


def turn(value, step):
    return lax.rem(value + step + 4, 4)


def dev_at(a, b, c):
    return ((b * (1 - c) + a * c) * 4 + a * (1 - c) + b * c) * 2 + c


def around(value):
    return [value, turn(value, -1), turn(value, 1), turn(value, 2)]


def normalize(rows, gain):
    wide = rows.astype(F32)
    inverse = lax.rsqrt(jnp.mean(wide * wide, axis=-1, keepdims=True) + EPSILON)
    return (wide * inverse * gain).astype(BF16)


def remote(src, dst, s, q, to):
    return pltpu.make_async_remote_copy(
        src_ref=src, dst_ref=dst, send_sem=s, recv_sem=q, device_id=to, device_id_type=MESH)


def span(first, size):
    return pl.ds(pl.multiple_of(first, 16), size)


def layer_kernel(
    near_ref, states, gain, labels, wq_hbm, wk_hbm, wv_hbm, wo_hbm, cot_hbm,
    branch, grad_states, summed,
    wq, wk, wv, wo, cot, marks, g, gl, far, fl, table,
    normed, q_own, d_att, keys, normed_keys, values, key_marks, bias,
    q_wide, d_wide, scores, d_probs, probs, d_scores, att, dq, kv_grad,
    parts, far_two, far_parts, base_t,
    give, take, far_send, far_recv, near_send, near_recv, line,
    far2_recv, near2_send, near2_recv, z_part, total,
    grads, g_mate, g_half, gz_recv, g_plane, gp_recv,
    load_s, as_, ar, mate_s, mate_r, ls, lr, zs, zr,
    give_s, take_s, s1s, s1r, s2s, s2r, gs, gr,
):
    r, c, a, b = place()
    d = lax.axis_index("dev")
    x, y = lax.rem(lax.div(d, 2), 4), lax.div(d, 8)
    ak, bk, rk = around(a), around(b), around(r)
    mate = (r, d + 1 - 2 * c)
    a_to = [(r, dev_at(k, b, c)) for k in ak]
    b_to = [(r, dev_at(a, k, c)) for k in bk]
    z_to = [(k, d) for k in rk]

    def peer_at(q):
        return (r, (turn(y, lax.div(q, 4)) * 4 + turn(x, lax.rem(q, 4))) * 2 + c)

    loads = []
    for n, (src, dst) in enumerate(((wq_hbm, wq), (cot_hbm, cot), (wo_hbm, wo), (wk_hbm, wk), (wv_hbm, wv))):
        load = pltpu.make_async_copy(src, dst, load_s.at[n])
        load.start()
        loads.append(load)
    barrier = pltpu.get_barrier_semaphore()
    for peer in [mate] + z_to[1:]:
        pl.semaphore_signal(barrier, inc=1, device_id=peer, device_id_type=MESH)

    def greet(q, _):
        pl.semaphore_signal(barrier, inc=1, device_id=peer_at(q), device_id_type=MESH)
        return 0

    lax.fori_loop(1, 16, greet, 0)
    marks[...] = jnp.zeros((8, 128), jnp.int32)
    marks[:2] = labels[...]
    pl.semaphore_wait(barrier, 19)
    started = []

    def send(src, dst, s, q, to):
        copy = remote(src, dst, s, q, to)
        copy.start()
        started.append(copy)

    def got(dst, s, q):
        remote(dst, dst, s, q, mate).wait_recv()

    def gather():
        def slot(i, j):
            return g.at[c, bk[j], ak[i]]

        def run(n, src, dst, to):
            send(src, dst, as_.at[n], ar.at[n], to)

        def arrived(n, dst):
            got(dst, as_.at[n], ar.at[n])

        def cross(i, j):
            src = states if i == 0 and j == 0 else slot(i, j)
            send(src, slot(i, j), mate_s.at[i * 4 + j], mate_r.at[i * 4 + j], mate)

        run(0, states, slot(0, 0), a_to[2])
        run(1, states, slot(0, 0), a_to[1])
        run(4, states, slot(0, 0), b_to[2])
        run(5, states, slot(0, 0), b_to[1])
        row = gl.at[c, b, a]
        send(marks, row, ls.at[0], lr.at[0], a_to[2])
        send(marks, row, ls.at[1], lr.at[1], a_to[1])
        send(states, far, zs.at[0], zr.at[0], z_to[1])
        send(marks, fl, zs.at[1], zr.at[1], z_to[1])
        cross(0, 0)
        g[c, b, a] = states[...]
        gl[c, b, a] = marks[...]
        yield
        arrived(0, slot(1, 0))
        run(2, slot(1, 0).at[0], slot(1, 0).at[0], a_to[2])
        run(8, slot(1, 0), slot(1, 0), b_to[2])
        run(9, slot(1, 0), slot(1, 0), b_to[1])
        arrived(1, slot(2, 0))
        run(3, slot(2, 0).at[1], slot(2, 0).at[1], a_to[1])
        run(12, slot(2, 0), slot(2, 0), b_to[2])
        run(13, slot(2, 0), slot(2, 0), b_to[1])

        def second(i):
            n = 4 + 4 * i
            arrived(n, slot(i, 1))
            run(n + 2, slot(i, 1).at[0], slot(i, 1).at[0], b_to[2])
            arrived(n + 1, slot(i, 2))
            run(n + 3, slot(i, 2).at[1], slot(i, 2).at[1], b_to[1])
            cross(i, 1)
            cross(i, 2)

        second(0)
        cross(1, 0)
        cross(2, 0)
        got(gl.at[c, b, ak[1]], ls.at[0], lr.at[0])
        send(gl.at[c, b, ak[1]], gl.at[c, b, ak[1]], ls.at[2], lr.at[2], a_to[2])
        got(gl.at[c, b, ak[2]], ls.at[1], lr.at[1])
        yield
        arrived(2, slot(3, 0).at[0])
        arrived(3, slot(3, 0).at[1])
        run(16, slot(3, 0), slot(3, 0), b_to[2])
        run(17, slot(3, 0), slot(3, 0), b_to[1])
        cross(3, 0)
        got(gl.at[c, b, ak[3]], ls.at[2], lr.at[2])
        send(gl.at[c, b], gl.at[c, b], ls.at[3], lr.at[3], b_to[2])
        send(gl.at[c, b], gl.at[c, b], ls.at[4], lr.at[4], b_to[1])
        yield
        second(1)
        yield
        second(2)
        got(gl.at[c, bk[1]], ls.at[3], lr.at[3])
        send(gl.at[c, bk[1]], gl.at[c, bk[1]], ls.at[5], lr.at[5], b_to[2])
        got(gl.at[c, bk[2]], ls.at[4], lr.at[4])
        yield
        second(3)
        got(gl.at[c, bk[3]], ls.at[5], lr.at[5])
        send(gl.at[c], gl.at[c], ls.at[6], lr.at[6], mate)
        for i in range(4):
            n = 4 + 4 * i
            arrived(n + 2, slot(i, 3).at[0])
            arrived(n + 3, slot(i, 3).at[1])
            cross(i, 3)
        for i in range(4):
            for j in range(4):
                got(g.at[1 - c, ak[j], bk[i]], mate_s.at[i * 4 + j], mate_r.at[i * 4 + j])
        got(gl.at[1 - c], ls.at[6], lr.at[6])
        yield

    gain_row = gain[...]

    def own_rows():
        for n in range(3):
            loads[n].wait()
        for k in range(2):
            rows = slice(k * 128, (k + 1) * 128)
            normed[rows] = normalize(states[k], gain_row)
            normed_keys[k, :128] = normed[rows]
        q_own[...] = (dot(normed[...], wq[...]).astype(BF16) * 0.125).astype(BF16)
        d_att[...] = dot(cot[...], wo[...], NT).astype(BF16)

    def project(k, rows):
        n = normed_keys[k, rows]
        keys[k, rows] = dot(n, wk[...]).astype(BF16)
        values[k, rows] = dot(n, wv[...]).astype(BF16)

    def own_keys():
        for n in (3, 4):
            loads[n].wait()
        for k in range(2):
            project(k, slice(0, 128))
            key_marks[k, :, :128] = jnp.broadcast_to(marks[k : k + 1], (8, 128)).astype(F32)

    def far_keys():
        got(far, zs.at[0], zr.at[0])
        got(fl, zs.at[1], zr.at[1])
        for k in range(2):
            m = lax.rem(near_ref[k, 5], 2)
            normed_keys[k, 640:] = normalize(far[m], gain_row)
            project(k, slice(640, 768))
            key_marks[k, :, 640:] = jnp.broadcast_to(fl[pl.ds(m, 1)], (8, 128)).astype(F32)

    def plan_parts():
        wanted = [lax.rem(near_ref[k, 1 + e], 64) for k in range(2) for e in range(4)]

        def look(t, _):
            found = jnp.int32(8)
            for n, block in enumerate(wanted):
                found = jnp.where(block == t, n, found)
            table[t] = found
            return 0

        lax.fori_loop(0, 64, look, 0)
        parts[8] = jnp.zeros((512, 128), BF16)

    def fetch(k, e):
        block = near_ref[k, 1 + e]
        at = lax.rem(lax.div(block, 2), 32)
        core = lax.rem(at, 2)
        ax = lax.rem(lax.div(at, 2), 4)
        ay = lax.div(at, 8)
        first, second = ax * (1 - core) + ay * core, ay * (1 - core) + ax * core
        local = lax.rem(block, 2)
        rows = slice((1 + e) * 128, (2 + e) * 128)
        normed_keys[k, rows] = normalize(g[core, second, first, local], gain_row)
        key_marks[k, :, rows] = jnp.broadcast_to(gl[core, second, first, pl.ds(local, 1)], (8, 128)).astype(F32)

    def fetched_keys():
        for k in range(2):
            for e in range(4):
                fetch(k, e)
        for k in range(2):
            def one(e, _, k=k):
                project(k, span(128 + e * 256, 256))
                return 0

            lax.fori_loop(0, 2, one, 0)
        for k in range(2):
            own = jnp.broadcast_to(marks[k : k + 1], (128, 128)).astype(F32).T
            for e in range(6):
                at = slice(e * 128, (e + 1) * 128)
                gap = jnp.abs(own - jnp.broadcast_to(key_marks[k, :1, at], (128, 128)))
                bias[k, :, at] = jnp.where(gap <= 1.0, 0.0, -jnp.inf)

    head_of = lax.broadcasted_iota(jnp.int32, (128, 256), 1) // 64

    def attend(n, _):
        k, half = lax.div(n, 2), lax.rem(n, 2)
        rows = pl.ds(pl.multiple_of(k * 128, 128), 128)
        cols = pl.ds(pl.multiple_of(half * 256, 256), 256)
        for i in range(4):
            at = slice(i * 128, (i + 1) * 128)
            q_wide[at] = jnp.where(head_of == i, q_own[rows, cols].astype(F32), 0.0).astype(BF16)
            d_wide[at] = jnp.where(head_of == i, d_att[rows, cols].astype(F32), 0.0).astype(BF16)
        scores[...] = dot(q_wide[...], keys[k, :, cols], NT)
        d_probs[...] = dot(d_wide[...], values[k, :, cols], NT)

        def soft(t, _):
            at = pl.ds(pl.multiple_of(t * 128, 128), 128)
            w = jnp.exp(scores[at] + bias[k])
            p = w * (1.0 / jnp.sum(w, axis=-1, keepdims=True))
            dp = d_probs[at]
            mean = jnp.sum(p * dp, axis=-1, keepdims=True)
            probs[at] = p.astype(BF16)
            d_scores[at] = (p * (dp - mean)).astype(BF16)
            return 0

        lax.fori_loop(0, 4, soft, 0, unroll=2)
        mixed = dot(probs[...], values[k, :, cols])
        turned = dot(d_scores[...], keys[k, :, cols])
        one = jnp.zeros((128, 256), F32)
        two = jnp.zeros((128, 256), F32)
        for i in range(4):
            at = slice(i * 128, (i + 1) * 128)
            one = one + jnp.where(head_of == i, mixed[at], 0.0)
            two = two + jnp.where(head_of == i, turned[at], 0.0)
        att[rows, cols] = one.astype(BF16)
        dq[rows, cols] = (two * 0.125).astype(BF16)
        kv_grad[k, cols] = dot(q_wide[...], d_scores[...], TN).astype(BF16)
        kv_grad[k, pl.ds(pl.multiple_of(512 + half * 256, 256), 256)] = dot(d_wide[...], probs[...], TN).astype(BF16)
        return 0

    def hold(p, m, value):
        for half in range(2):
            grads[p, pl.ds(m * 1024 + half * 512, 512)] = value[:, half * 256 : (half + 1) * 256].astype(BF16)

    def query_output():
        hold(0, 0, dot(normed[...], dq[...], TN))
        hold(0, 1, dot(att[...], cot[...], TN))

    def key_value():
        for m in range(2):
            at = slice(m * 512, (m + 1) * 512)
            hold(1, m, (dot(kv_grad[0, at], normed_keys[0]) + dot(kv_grad[1, at], normed_keys[1])).T)

    def part_of(k, at):
        return dot(wk[...], kv_grad[k, :512, at]) + dot(wv[...], kv_grad[k, 512:, at])

    def near_parts(k):
        for pair in range(2):
            value = part_of(k, slice(128 + pair * 256, 384 + pair * 256)).astype(BF16)
            for e in range(2):
                parts[k * 4 + pair * 2 + e] = value[:, e * 128 : (e + 1) * 128]

    def edge_parts():
        for k in range(2):
            far_two[k] = part_of(k, slice(640, 768)).astype(BF16)
        m = lax.rem(near_ref[0, 5], 2)
        for k in range(2):
            far_parts[k] = far_two[lax.rem(k + m, 2)]
        send(far_parts, z_part, zs.at[2], zr.at[2], z_to[2])

    def own_parts():
        mine = dot(wq[...], dq[...], NT)
        for k in range(2):
            at = slice(k * 128, (k + 1) * 128)
            base_t[:, at] = mine[:, at] + part_of(k, slice(0, 128)).astype(BF16).astype(F32)
        branch[...] = dot(att[...], wo[...]).astype(BF16)

    def each(work):
        def step(t, _):
            work(pl.ds(pl.multiple_of(t * 128, 128), 128))
            return 0

        lax.fori_loop(0, 4, step, 0)

    def here(i, j, block, rows):
        mine = parts[table[2 * dev_at(ak[i], bk[j], c) + block], rows]
        return mine.astype(F32) + take[i * 4 + j, block, rows].astype(F32)

    def took(i, j):
        got(take.at[i * 4 + j], give_s.at[i * 4 + j], take_s.at[i * 4 + j])

    order = (3, 1, 2, 0)

    def exchange(j):
        for i in order:
            n = i * 4 + j
            for block in range(2):
                give[n, block] = parts[table[2 * dev_at(bk[i], ak[j], 1 - c) + block]]
            send(give.at[n], take.at[n], give_s.at[n], take_s.at[n], mate)

    def rings():
        for i in order:
            took(i, 3)
            for block in range(2):
                def far_sum(rows, block=block, i=i):
                    far_send[i, block, rows] = here(i, 3, block, rows).astype(BF16)

                each(far_sum)
                send(far_send.at[i, block], far_recv.at[i, block], s1s.at[i * 4 + block], s1r.at[i * 4 + block], b_to[2 - block])
        yield
        for i in order:
            for way in range(2):
                j = 2 - way
                took(i, j)
                got(far_recv.at[i, way], s1s.at[i * 4 + way], s1r.at[i * 4 + way])

                def near_sum(rows, way=way, i=i, j=j):
                    near_send[i, way, way, rows] = (here(i, j, way, rows) + far_recv[i, way, rows].astype(F32)).astype(BF16)
                    near_send[i, way, 1 - way, rows] = here(i, j, 1 - way, rows).astype(BF16)

                each(near_sum)
                send(near_send.at[i, way], near_recv.at[i, way], s1s.at[i * 4 + 2 + way], s1r.at[i * 4 + 2 + way], b_to[j])
            yield

        def ring_end(i):
            took(i, 0)
            for way in range(2):
                got(near_recv.at[i, way], s1s.at[i * 4 + 2 + way], s1r.at[i * 4 + 2 + way])
            for block in range(2):
                def end(rows, block=block):
                    line[i, block, rows] = (
                        here(i, 0, block, rows) + near_recv[i, 0, block, rows].astype(F32)
                        + near_recv[i, 1, block, rows].astype(F32)).astype(BF16)

                each(end)

        ring_end(3)
        for block in range(2):
            send(line.at[3, block], far2_recv.at[block], s2s.at[block], s2r.at[block], a_to[2 - block])
        yield
        for way in (1, 0):
            ring_end(2 - way)
            got(far2_recv.at[way], s2s.at[way], s2r.at[way])

            def near2(rows, way=way):
                near2_send[way, way, rows] = (line[2 - way, way, rows].astype(F32) + far2_recv[way, rows].astype(F32)).astype(BF16)
                near2_send[way, 1 - way, rows] = line[2 - way, 1 - way, rows]

            each(near2)
            send(near2_send.at[way], near2_recv.at[way], s2s.at[2 + way], s2r.at[2 + way], a_to[2 - way])
            yield
        ring_end(0)
        yield
        for way in range(2):
            got(near2_recv.at[way], s2s.at[2 + way], s2r.at[2 + way])
        got(z_part, zs.at[2], zr.at[2])
        for block in range(2):
            def last(rows, block=block):
                at = slice(block * 128, block * 128 + 128)
                total[rows, at] = (
                    base_t[rows, at] + line[0, block, rows].astype(F32) + near2_recv[0, block, rows].astype(F32)
                    + near2_recv[1, block, rows].astype(F32) + z_part[block, rows].astype(F32))

            each(last)
        for block in range(2):
            rows = slice(block * 128, block * 128 + 128)
            d_normed = total[:, rows].T
            wide = states[block].astype(F32)
            inverse = lax.rsqrt(jnp.mean(wide * wide, axis=-1, keepdims=True) + EPSILON)
            scaled = d_normed * gain_row
            along = jnp.sum(scaled * wide, axis=-1, keepdims=True) * (1.0 / 512)
            grad_states[rows] = (inverse * scaled - wide * (inverse * inverse * inverse * along)).astype(BF16)
        yield

    base = c * 1024

    def chunk_at(q):
        return (turn(y, lax.div(q, 4)) * 4 + turn(x, lax.rem(q, 4))) * 16

    def other_way(q):
        return lax.rem(4 - lax.div(q, 4), 4) * 4 + lax.rem(4 - lax.rem(q, 4), 4)

    def weights(p):
        at = p * 38
        whole = summed.at[p]
        send(grads.at[p, span(1024 - base, 1024)], g_mate.at[p], gs.at[at], gr.at[at], mate)
        yield
        got(g_mate.at[p], gs.at[at], gr.at[at])

        def half_sum(t, _):
            rows = span(t * 128, 128)
            g_half[p, rows] = (grads[p, span(base + t * 128, 128)].astype(F32) + g_mate[p, rows].astype(F32)).astype(BF16)
            return 0

        lax.fori_loop(0, 8, half_sum, 0)
        for k in range(1, 4):
            send(g_half.at[p, span(rk[k] * 256, 256)], gz_recv.at[p, k - 1], gs.at[at + k], gr.at[at + k], z_to[k])
        yield
        for k in range(1, 4):
            got(gz_recv.at[p, k - 1], gs.at[at + k], gr.at[at + k])

        def z_sum(t, _):
            rows = span(t * 64, 64)
            g_plane[p, rows] = (
                g_half[p, span(r * 256 + t * 64, 64)].astype(F32) + gz_recv[p, 0, rows].astype(F32)
                + gz_recv[p, 1, rows].astype(F32) + gz_recv[p, 2, rows].astype(F32)).astype(BF16)
            return 0

        lax.fori_loop(0, 4, z_sum, 0)

        def plane_out(q):
            return remote(
                g_plane.at[p, span(chunk_at(q), 16)], gp_recv.at[p, q - 1],
                gs.at[at + 3 + q], gr.at[at + 3 + q], peer_at(q))

        def begin(q, _):
            plane_out(q).start()
            return 0

        lax.fori_loop(1, 16, begin, 0)
        yield

        def plane_sum(q, held):
            plane_out(q).wait()
            return held + gp_recv[p, q - 1].astype(F32)

        held = lax.fori_loop(1, 16, plane_sum, g_plane[p, span(chunk_at(0), 16)].astype(F32))
        mine = span(base + r * 256 + chunk_at(0), 16)
        summed[p, mine] = held.astype(BF16)

        def back_out(q):
            return remote(whole.at[mine], whole.at[mine], gs.at[at + 18 + q], gr.at[at + 18 + q], peer_at(q))

        def begin_back(q, _):
            back_out(q).start()
            return 0

        lax.fori_loop(1, 16, begin_back, 0)
        yield

        def end_back(q, _):
            back_out(q).wait_send()
            there = whole.at[span(base + r * 256 + chunk_at(other_way(q)), 16)]
            remote(there, there, gs.at[at + 18 + q], gr.at[at + 18 + q], mate).wait_recv()
            return 0

        lax.fori_loop(1, 16, end_back, 0)
        line_part = whole.at[span(base + r * 256, 256)]
        for k in range(1, 4):
            send(line_part, line_part, gs.at[at + 33 + k], gr.at[at + 33 + k], z_to[k])
        yield
        for k, source in ((1, rk[2]), (2, rk[1]), (3, rk[3])):
            got(whole.at[span(base + source * 256, 256)], gs.at[at + 33 + k], gr.at[at + 33 + k])
        half = whole.at[span(base, 1024)]
        send(half, half, gs.at[at + 37], gr.at[at + 37], mate)
        yield
        got(whole.at[span(1024 - base, 1024)], gs.at[at + 37], gr.at[at + 37])
        yield

    states_in, first, second, ring = gather(), weights(0), weights(1), rings()
    next(states_in)
    own_rows()
    own_keys()
    plan_parts()
    next(states_in)
    far_keys()
    for _ in range(4):
        next(states_in)
    fetched_keys()
    lax.fori_loop(0, 4, attend, 0)
    query_output()
    next(first)
    near_parts(0)
    near_parts(1)
    next(first)
    for j in (3, 1, 2, 0):
        exchange(j)
    key_value()
    next(second)
    next(ring)
    next(first)
    edge_parts()
    next(second)
    next(ring)
    next(first)
    own_parts()
    for step in PLAN:
        next({"w": first, "v": second, "r": ring}[step])
    for copy in started:
        copy.wait_send()


PLAN = "rrwvrrwvrrwrrvvv"


def layer(neighbours, states, gain, labels, wq, wk, wv, wo, cot):
    vmem = pl.BlockSpec(memory_space=pltpu.VMEM)
    smem = pl.BlockSpec(memory_space=pltpu.SMEM)
    anywhere = pl.BlockSpec(memory_space=pl.ANY)
    dma = pltpu.SemaphoreType.DMA

    def half(*shape):
        return pltpu.VMEM(shape, BF16)

    def full(*shape):
        return pltpu.VMEM(shape, F32)

    def whole(*shape):
        return pltpu.VMEM(shape, jnp.int32)

    return pl.pallas_call(
        layer_kernel,
        out_shape=(
            jax.ShapeDtypeStruct((256, 512), BF16),
            jax.ShapeDtypeStruct((256, 512), BF16),
            jax.ShapeDtypeStruct((2, 2048, 256), BF16),
        ),
        in_specs=[smem] + [vmem] * 3 + [anywhere] * 5,
        out_specs=[vmem] * 3,
        scratch_shapes=[
            half(512, 512), half(512, 512), half(512, 512), half(512, 512), half(256, 512),
            whole(8, 128), half(2, 4, 4, 2, 128, 512), whole(2, 4, 4, 8, 128), half(2, 128, 512), whole(8, 128),
            pltpu.SMEM((64,), jnp.int32),
            half(256, 512), half(256, 512), half(256, 512),
            half(2, 768, 512), half(2, 768, 512), half(2, 768, 512), full(2, 8, 768), full(2, 128, 768),
            half(512, 256), half(512, 256), full(512, 768), full(512, 768), half(512, 768), half(512, 768),
            half(256, 512), half(256, 512), half(2, 1024, 768),
            half(9, 512, 128), half(2, 512, 128), half(2, 512, 128), full(512, 256),
            half(16, 2, 512, 128), half(16, 2, 512, 128),
            half(4, 2, 512, 128), half(4, 2, 512, 128),
            half(4, 2, 2, 512, 128), half(4, 2, 2, 512, 128), half(4, 2, 512, 128),
            half(2, 512, 128), half(2, 2, 512, 128), half(2, 2, 512, 128), half(2, 512, 128), full(512, 256),
            half(2, 2048, 256), half(2, 1024, 256), half(2, 1024, 256), half(2, 3, 256, 256),
            half(2, 256, 256), half(2, 15, 16, 256),
            dma((5,)), dma((20,)), dma((20,)), dma((16,)), dma((16,)), dma((7,)), dma((7,)), dma((3,)), dma((3,)),
            dma((16,)), dma((16,)), dma((16,)), dma((16,)), dma((4,)), dma((4,)), dma((76,)), dma((76,)),
        ],
        compiler_params=pltpu.CompilerParams(collective_id=0, has_side_effects=True, vmem_limit_bytes=VMEM_LIMIT),
    )(neighbours, states, gain, labels, wq, wk, wv, wo, cot)


def body(states, norm_gain, w_query, w_key, w_value, w_out, neighbours, labels, cotangent):
    branch_out, grad_states, summed = layer(
        neighbours, states.reshape(2, 128, 512), norm_gain.reshape(1, -1), labels, w_query, w_key, w_value, w_out, cotangent)
    scale = 1.0 / math.sqrt(32768)
    split = summed.reshape(2, 2, 2, 512, 256)

    def joined(p, m):
        return jnp.concatenate([split[p, m, 0], split[p, m, 1]], axis=1).astype(F32) * scale

    grad_query, grad_output, grad_key, grad_value = joined(0, 0), joined(0, 1), joined(1, 0), joined(1, 1)
    along = grad_query * w_query.astype(F32) + grad_key * w_key.astype(F32) + grad_value * w_value.astype(F32)
    grad_gain = jnp.sum(along, axis=1) / norm_gain
    return branch_out, grad_states, grad_query, grad_key, grad_value, grad_output, grad_gain


def solution(mesh):
    rows = P(("region", "dev"), None)
    return jax.shard_map(
        body, mesh=mesh,
        in_specs=(rows, P(), P(), P(), P(), P(), rows, rows, rows),
        out_specs=(rows, rows, P(), P(), P(), P(), P()),
        check_vma=False)
```

time: 491 us -> 108 us (0.22)
  waiting for transfers between devices: 225 us -> 0 us
  Pallas kernels: 0 us -> 100 us
  blocking collectives: 70.4 us -> 0 us
  local copies, waits for them, and re-layouts: 68.2 us -> 3.37 us
  matrix products: 53.2 us -> 0 us
  starting transfers between devices: 36.5 us -> 0 us
  other arithmetic: 22.3 us -> 3.1 us
  between operations: 14.6 us -> 0.68 us
    all_to_all x4 -> x0, waiting for transfers between devices: 149 us -> none  [the longest x3 147 us: across_dev(): lax.all_to_all(shortened(parcel), 'dev', split_axis=0, concat_axis=0, til...]
    pallas_call x0 -> x1, Pallas kernels: none -> 100 us  [layer(): pl.pallas_call(layer_kernel, out_shape=(jax.ShapeDtypeStruct((256, 512),...]
    psum x1 -> x0, blocking collectives: 70.4 us -> none  [body(): lax.psum((grad_query, grad_pairs[:, :model_width], grad_pairs[:, model_wi...]
    psum x1 -> x0, waiting for transfers between devices: 65.3 us -> none  [body(): lax.psum((grad_query, grad_pairs[:, :model_width], grad_pairs[:, model_wi...]
    dot_general x18 -> x0, matrix products: 53.2 us -> none  [the longest x3 11.9 us: attend(): jnp.einsum('qhd,khd->hqk', query_heads, key_heads, preferred_element_type...]
    all_to_all x4 -> x0, starting transfers between devices: 30.3 us -> none  [the longest x3 21.7 us: across_dev(): lax.all_to_all(shortened(parcel), 'dev', split_axis=0, concat_axis=0, til...]
    gather x17 -> x0, local copies, waits for them, and re-layouts: 28.9 us -> none  [the longest x2 9.42 us: body(): normed_blocks[served]]
    slice x9 -> x0, local copies, waits for them, and re-layouts: 10.8 us -> none  [the longest x2 2.99 us: attend(): key_heads = key_pairs[:, :model_width].reshape(key_count, HEADS, head_dim)]
  transfers between devices with their start and end apart: 8 -> 0, of which waited for: 7 -> 0; matrix products, arithmetic and copies ran while one was open for 14% -> 0% of each run, Pallas kernels for 0% -> 0%
where the time goes in v2:
time: 108 us; the launch traced here: 107 us
  Pallas kernels  100 us (93%)
  local copies, waits for them, and re-layouts  3.37 us (3%)
  other arithmetic  3.1 us (3%)
    pallas_call x1, Pallas kernels, layer(): pl.pallas_call(layer_kernel, out_shape=(jax.ShapeDtypeStruct((256, 512),...  100 us
    reduce_sum x1, other arithmetic, body(): grad_gain = jnp.sum(along, axis=1) / norm_gain  2.51 us

profile of v2, /device:TPU:1, one launch (start us, length us, event | category | flops | bytes accessed | tf_op | source)
XLA Modules:
  0.0 107.5 jit_solution(6098666401019252760)
XLA Ops:
  0.6 100.3 %shard_map.144 = (bf16[256,512]{1,0:T(8,128)(2,1)}, bf16[256,512]{1,0:T(8,128)(2,1)}, bf16[2,2048,256]{2,1,0:T(8,128)(2,1)}) custom-call(s32[2,6]{1,0:T(2,128)} %near_ref.1, bf16[2,128,512]{2,1,0:T(8,128)(2,1)} %bitcast.20, f32[1,512]{1,0:T(1,128)} %bitcast.21, s32[2,128]{1,0:T(2,128)} %labels.1, bf16[512,512]{1,0:T(8,128)(2,1)} %wq_hbm.1, ...), custom_call_target="tpu_custom_call" | custom-call | tf_op jit(solution)/shard_map/pallas_call | solution.py:578
  101.0 0.0 copy-start
  101.0 0.0 copy-start.1
  101.0 0.0 copy-start.2
  101.0 1.8 %slice_bitcast_fusion.1 = (bf16[512,256]{1,0:T(8,128)(2,1)S(1)}, bf16[512,256]{1,0:T(8,128)(2,1)S(1)}, bf16[512,256]{1,0:T(8,128)(2,1)S(1)}, bf16[512,256]{1,0:T...) fusion(bf16[2,2,2,512,256]{4,3,2,1,0:T(8,128)(2,1)} %bitcast.19), kind=kLoop, calls=%fused_computation.6 | loop fusion | bytes 4194304 | tf_op jit(solution)/shard_map/squeeze | solution.py:616
  102.8 0.0 copy-done
  102.8 0.0 copy-done.1
  102.8 0.2 copy-done.2
  103.0 0.0 copy-start.5
  103.0 0.0 copy-start.4
  103.0 0.0 copy-start.3
  103.0 2.5 %add_reduce_fusion = (f32[512]{0:T(512)S(1)}, f32[512,512]{1,0:T(8,128)}, f32[512,512]{1,0:T(8,128)}, f32[512,512]{1,0:T(8,128)}, f32[512,512]{1,0:T(8,128)}) fusion(bf16[512,512]{1,0:T(8,128)(2,1)S(1)} %copy-done.2, bf16[512,512]{1,0:T(8,128)(2,1)S(1)} %copy-done.1, bf16[512,512]{1,0:T(8,128)(2,1)S(1)} %copy-done, bf16[512,256]{1,0:T(8,128)(2,1)S(1)} %get-tuple-element.19, ...), kind=kLoop, calls=%fused_computation | loop fusion | flops 7601664 | bytes 7866368 | tf_op jit(solution)/shard_map/reduce_sum | solution.py:620
  105.5 0.0 copy-done.5
  105.5 0.6 div.3
  106.1 0.0 copy-done.4
  106.1 0.7 copy.18
  106.8 0.0 copy-done.3
  106.8 0.7 copy.19
Async XLA Ops:
  101.0 1.8 %copy-start = (bf16[512,512]{1,0:T(8,128)(2,1)S(1)}, bf16[512,512]{1,0:T(8,128)(2,1)}, u32[]{:S(2)}) copy-start(bf16[512,512]{1,0:T(8,128)(2,1)} %wq_hbm.1) | copy-start | bytes 1572868
  101.0 1.8 %copy-start.1 = (bf16[512,512]{1,0:T(8,128)(2,1)S(1)}, bf16[512,512]{1,0:T(8,128)(2,1)}, u32[]{:S(2)}) copy-start(bf16[512,512]{1,0:T(8,128)(2,1)} %wk_hbm.1) | copy-start | bytes 1572868
  101.0 2.0 %copy-start.2 = (bf16[512,512]{1,0:T(8,128)(2,1)S(1)}, bf16[512,512]{1,0:T(8,128)(2,1)}, u32[]{:S(2)}) copy-start(bf16[512,512]{1,0:T(8,128)(2,1)} %wv_hbm.1) | copy-start | bytes 1572868
  103.0 2.5 %copy-start.5 = (f32[512]{0:T(512)S(1)}, f32[512]{0:T(512)}, u32[]{:S(2)}) copy-start(f32[512]{0:T(512)} %param.10) | copy-start | bytes 6148
  103.0 3.1 %copy-start.4 = (bf16[256,512]{1,0:T(8,128)(2,1)S(1)}, bf16[256,512]{1,0:T(8,128)(2,1)}, u32[]{:S(2)}) copy-start(bf16[256,512]{1,0:T(8,128)(2,1)} %get-tuple-element.33) | copy-start | bytes 786436
  103.0 3.8 %copy-start.3 = (bf16[256,512]{1,0:T(8,128)(2,1)S(1)}, bf16[256,512]{1,0:T(8,128)(2,1)}, u32[]{:S(2)}) copy-start(bf16[256,512]{1,0:T(8,128)(2,1)} %get-tuple-element.34) | copy-start | bytes 786436

commit v3 on v2

--- a/solution.py
+++ b/solution.py
@@ -114,20 +114,40 @@
         def slot(i, j):
             return g.at[c, bk[j], ak[i]]
 
-        def run(n, src, dst, to):
+        def first_in(n, i, half):
+            got(slot(i, 0).at[half], as_.at[n], ar.at[n])
+
+        def out(n, src, dst, to):
             send(src, dst, as_.at[n], ar.at[n], to)
-
-        def arrived(n, dst):
-            got(dst, as_.at[n], ar.at[n])
 
         def cross(i, j):
             src = states if i == 0 and j == 0 else slot(i, j)
             send(src, slot(i, j), mate_s.at[i * 4 + j], mate_r.at[i * 4 + j], mate)
 
-        run(0, states, slot(0, 0), a_to[2])
-        run(1, states, slot(0, 0), a_to[1])
-        run(4, states, slot(0, 0), b_to[2])
-        run(5, states, slot(0, 0), b_to[1])
+        def second_out(i, half, way):
+            src = states if i == 0 else slot(i, 0)
+            out(6 + 6 * i + 2 * way + half, src.at[half], slot(i, 0).at[half], b_to[2 - way])
+
+        def second_in(i, half, way):
+            n = 6 + 6 * i + 2 * way + half
+            got(slot(i, 1 + way).at[half], as_.at[n], ar.at[n])
+
+        def second_on(i, way):
+            second_in(i, way, way)
+            there = slot(i, 1 + way).at[way]
+            out(10 + 6 * i + way, there, there, b_to[2 - way])
+
+        def first_on(way):
+            first_in(2 * way + way, 1 + way, way)
+            there = slot(1 + way, 0).at[way]
+            out(4 + way, there, there, a_to[2 - way])
+
+        for block in range(2):
+            for way in range(2):
+                half = block if way == 0 else 1 - block
+                out(2 * way + half, states.at[half], slot(0, 0).at[half], a_to[2 - way])
+            for way in range(2):
+                second_out(0, block if way == 0 else 1 - block, way)
         row = gl.at[c, b, a]
         send(marks, row, ls.at[0], lr.at[0], a_to[2])
         send(marks, row, ls.at[1], lr.at[1], a_to[1])
@@ -137,54 +157,56 @@
         g[c, b, a] = states[...]
         gl[c, b, a] = marks[...]
         yield
-        arrived(0, slot(1, 0))
-        run(2, slot(1, 0).at[0], slot(1, 0).at[0], a_to[2])
-        run(8, slot(1, 0), slot(1, 0), b_to[2])
-        run(9, slot(1, 0), slot(1, 0), b_to[1])
-        arrived(1, slot(2, 0))
-        run(3, slot(2, 0).at[1], slot(2, 0).at[1], a_to[1])
-        run(12, slot(2, 0), slot(2, 0), b_to[2])
-        run(13, slot(2, 0), slot(2, 0), b_to[1])
-
-        def second(i):
-            n = 4 + 4 * i
-            arrived(n, slot(i, 1))
-            run(n + 2, slot(i, 1).at[0], slot(i, 1).at[0], b_to[2])
-            arrived(n + 1, slot(i, 2))
-            run(n + 3, slot(i, 2).at[1], slot(i, 2).at[1], b_to[1])
-            cross(i, 1)
-            cross(i, 2)
-
-        second(0)
-        cross(1, 0)
-        cross(2, 0)
+        for way in range(2):
+            first_on(way)
+            second_out(1 + way, way, way)
+            second_out(1 + way, way, 1 - way)
+        for way in range(2):
+            second_on(0, way)
+        for way in range(2):
+            first_in(2 * way + 1 - way, 1 + way, 1 - way)
+            second_out(1 + way, 1 - way, 1 - way)
+            second_out(1 + way, 1 - way, way)
+            cross(1 + way, 0)
+        for way in range(2):
+            second_in(0, 1 - way, way)
+            cross(0, 1 + way)
         got(gl.at[c, b, ak[1]], ls.at[0], lr.at[0])
         send(gl.at[c, b, ak[1]], gl.at[c, b, ak[1]], ls.at[2], lr.at[2], a_to[2])
         got(gl.at[c, b, ak[2]], ls.at[1], lr.at[1])
         yield
-        arrived(2, slot(3, 0).at[0])
-        arrived(3, slot(3, 0).at[1])
-        run(16, slot(3, 0), slot(3, 0), b_to[2])
-        run(17, slot(3, 0), slot(3, 0), b_to[1])
+        for way in range(2):
+            got(slot(3, 0).at[way], as_.at[4 + way], ar.at[4 + way])
+            second_out(3, way, way)
+            second_out(3, way, 1 - way)
         cross(3, 0)
         got(gl.at[c, b, ak[3]], ls.at[2], lr.at[2])
         send(gl.at[c, b], gl.at[c, b], ls.at[3], lr.at[3], b_to[2])
         send(gl.at[c, b], gl.at[c, b], ls.at[4], lr.at[4], b_to[1])
         yield
-        second(1)
-        yield
-        second(2)
+        for way in range(2):
+            second_on(1 + way, way)
+        for way in range(2):
+            second_on(2 - way, way)
+        for i in (1, 2):
+            for way in range(2):
+                second_in(i, 1 - way, way)
+                cross(i, 1 + way)
+        yield
         got(gl.at[c, bk[1]], ls.at[3], lr.at[3])
         send(gl.at[c, bk[1]], gl.at[c, bk[1]], ls.at[5], lr.at[5], b_to[2])
         got(gl.at[c, bk[2]], ls.at[4], lr.at[4])
-        yield
-        second(3)
+        for way in range(2):
+            second_on(3, way)
+        for way in range(2):
+            second_in(3, 1 - way, way)
+            cross(3, 1 + way)
+        yield
         got(gl.at[c, bk[3]], ls.at[5], lr.at[5])
         send(gl.at[c], gl.at[c], ls.at[6], lr.at[6], mate)
         for i in range(4):
-            n = 4 + 4 * i
-            arrived(n + 2, slot(i, 3).at[0])
-            arrived(n + 3, slot(i, 3).at[1])
+            for way in range(2):
+                got(slot(i, 3).at[way], as_.at[10 + 6 * i + way], ar.at[10 + 6 * i + way])
             cross(i, 3)
         for i in range(4):
             for j in range(4):
@@ -375,6 +397,7 @@
                 each(far_sum)
                 send(far_send.at[i, block], far_recv.at[i, block], s1s.at[i * 4 + block], s1r.at[i * 4 + block], b_to[2 - block])
         yield
+        near_copies = []
         for i in order:
             for way in range(2):
                 j = 2 - way
@@ -386,8 +409,13 @@
                     near_send[i, way, 1 - way, rows] = here(i, j, 1 - way, rows).astype(BF16)
 
                 each(near_sum)
-                send(near_send.at[i, way], near_recv.at[i, way], s1s.at[i * 4 + 2 + way], s1r.at[i * 4 + 2 + way], b_to[j])
+                if len(near_copies) >= 2 * AHEAD:
+                    near_copies[-2 * AHEAD].wait_send()
+                copy = remote(near_send.at[i, way], near_recv.at[i, way], s1s.at[i * 4 + 2 + way], s1r.at[i * 4 + 2 + way], b_to[j])
+                copy.start()
+                near_copies.append(copy)
             yield
+        started.extend(near_copies[-2 * AHEAD :])
 
         def ring_end(i):
             took(i, 0)
@@ -535,29 +563,21 @@
         next(states_in)
     fetched_keys()
     lax.fori_loop(0, 4, attend, 0)
-    query_output()
-    next(first)
-    near_parts(0)
-    near_parts(1)
-    next(first)
-    for j in (3, 1, 2, 0):
-        exchange(j)
-    key_value()
-    next(second)
-    next(ring)
-    next(first)
-    edge_parts()
-    next(second)
-    next(ring)
-    next(first)
-    own_parts()
+    tasks = {
+        "Q": query_output, "K": key_value, "N": lambda: (near_parts(0), near_parts(1)), "E": edge_parts, "O": own_parts,
+        "w": lambda: next(first), "v": lambda: next(second), "r": lambda: next(ring),
+    }
     for step in PLAN:
-        next({"w": first, "v": second, "r": ring}[step])
+        if step in "0123":
+            exchange(int(step))
+        else:
+            tasks[step]()
     for copy in started:
         copy.wait_send()
 
 
-PLAN = "rrwvrrwvrrwrrvvv"
+AHEAD = 1
+PLAN = "QwKvN3wv12r0wrrEOwvrrvwrrrvrwrwvv"
 
 
 def layer(neighbours, states, gain, labels, wq, wk, wv, wo, cot):
@@ -599,26 +619,60 @@
             half(2, 512, 128), half(2, 2, 512, 128), half(2, 2, 512, 128), half(2, 512, 128), full(512, 256),
             half(2, 2048, 256), half(2, 1024, 256), half(2, 1024, 256), half(2, 3, 256, 256),
             half(2, 256, 256), half(2, 15, 16, 256),
-            dma((5,)), dma((20,)), dma((20,)), dma((16,)), dma((16,)), dma((7,)), dma((7,)), dma((3,)), dma((3,)),
+            dma((5,)), dma((30,)), dma((30,)), dma((16,)), dma((16,)), dma((7,)), dma((7,)), dma((3,)), dma((3,)),
             dma((16,)), dma((16,)), dma((16,)), dma((16,)), dma((4,)), dma((4,)), dma((76,)), dma((76,)),
         ],
         compiler_params=pltpu.CompilerParams(collective_id=0, has_side_effects=True, vmem_limit_bytes=VMEM_LIMIT),
     )(neighbours, states, gain, labels, wq, wk, wv, wo, cot)
 
 
+def finish_kernel(
+    sum_query, sum_key, sum_value, sum_output, wq, wk, wv, gain, branch_in, states_in,
+    branch, grad_states, grad_query, grad_key, grad_value, grad_output, grad_gain,
+):
+    branch[...] = branch_in[...]
+    grad_states[...] = states_in[...]
+    scale = 1.0 / math.sqrt(32768)
+    along = jnp.zeros((128, 256), F32)
+    for summed, weight, out in ((sum_query, wq, grad_query), (sum_key, wk, grad_key), (sum_value, wv, grad_value)):
+        for half in range(2):
+            cols = slice(half * 256, half * 256 + 256)
+            value = summed[0, 0, half].astype(F32) * scale
+            out[:, cols] = value
+            along = along + value * weight[:, cols].astype(F32)
+    for side in range(2):
+        grad_output[:, side * 256 : side * 256 + 256] = sum_output[0, 0, side].astype(F32) * scale
+    turned = (along[:, :128] + along[:, 128:]).T
+    grad_gain[...] = jnp.sum(turned, axis=0, keepdims=True) / gain[...]
+
+
+def finish(summed, wq, wk, wv, gain, branch, grad_states):
+    square = jax.ShapeDtypeStruct((512, 512), F32)
+    rows = jax.ShapeDtypeStruct((256, 512), BF16)
+    by_row = pl.BlockSpec((128, 512), lambda i: (i, 0))
+    thin = pl.BlockSpec((64, 512), lambda i: (i, 0))
+    line = pl.BlockSpec((1, 128), lambda i: (0, i))
+
+    def product(p, m):
+        return pl.BlockSpec((1, 1, 2, 128, 256), lambda i: (p, m, 0, i, 0))
+
+    by_product = summed.reshape(2, 2, 2, 512, 256)
+    return pl.pallas_call(
+        finish_kernel,
+        grid=(4,),
+        out_shape=(rows, rows, square, square, square, square, jax.ShapeDtypeStruct((1, 512), F32)),
+        in_specs=[product(0, 0), product(1, 0), product(1, 1), product(0, 1), by_row, by_row, by_row, line, thin, thin],
+        out_specs=[thin, thin, by_row, by_row, by_row, by_row, line],
+        compiler_params=pltpu.CompilerParams(vmem_limit_bytes=VMEM_LIMIT),
+    )(by_product, by_product, by_product, by_product, wq, wk, wv, gain, branch, grad_states)
+
+
 def body(states, norm_gain, w_query, w_key, w_value, w_out, neighbours, labels, cotangent):
+    gain = norm_gain.reshape(1, -1)
     branch_out, grad_states, summed = layer(
-        neighbours, states.reshape(2, 128, 512), norm_gain.reshape(1, -1), labels, w_query, w_key, w_value, w_out, cotangent)
-    scale = 1.0 / math.sqrt(32768)
-    split = summed.reshape(2, 2, 2, 512, 256)
-
-    def joined(p, m):
-        return jnp.concatenate([split[p, m, 0], split[p, m, 1]], axis=1).astype(F32) * scale
-
-    grad_query, grad_output, grad_key, grad_value = joined(0, 0), joined(0, 1), joined(1, 0), joined(1, 1)
-    along = grad_query * w_query.astype(F32) + grad_key * w_key.astype(F32) + grad_value * w_value.astype(F32)
-    grad_gain = jnp.sum(along, axis=1) / norm_gain
-    return branch_out, grad_states, grad_query, grad_key, grad_value, grad_output, grad_gain
+        neighbours, states.reshape(2, 128, 512), gain, labels, w_query, w_key, w_value, w_out, cotangent)
+    outs = finish(summed, w_query, w_key, w_value, gain, branch_out, grad_states)
+    return *outs[:6], outs[6].reshape(-1)
 
 
 def solution(mesh):

time: 108 us -> 101 us (0.935)
  local copies, waits for them, and re-layouts: 3.37 us -> 0 us
  other arithmetic: 3.1 us -> 0 us
    pallas_call x1, Pallas kernels: 100 us -> 94.6 us  [layer(): pl.pallas_call(layer_kernel, out_shape=(jax.ShapeDtypeStruct((256, 512),...]
    pallas_call x0 -> x1, Pallas kernels: none -> 5 us  [finish(): pl.pallas_call(finish_kernel, grid=(4,), out_shape=(rows, rows, square, s...]
    reduce_sum x1 -> x0, other arithmetic: 2.51 us -> none  [body(): grad_gain = jnp.sum(along, axis=1) / norm_gain]
    squeeze x1 -> x0, local copies, waits for them, and re-layouts: 1.75 us -> none  [joined(): split[p, m, 0]]
    unnamed x14 -> x0, local copies, waits for them, and re-layouts: 1.62 us -> none
where the time goes in v3:
time: 101 us; the launch traced here: 100 us
  Pallas kernels  99.6 us (99%)
    pallas_call x1, Pallas kernels, layer(): pl.pallas_call(layer_kernel, out_shape=(jax.ShapeDtypeStruct((256, 512),...  94.6 us
    pallas_call x1, Pallas kernels, finish(): pl.pallas_call(finish_kernel, grid=(4,), out_shape=(rows, rows, square, s...  5 us

profile of v3, /device:TPU:1, one launch (start us, length us, event | category | flops | bytes accessed | tf_op | source)
XLA Modules:
  0.0 100.3 jit_solution(2663714111168138313)
XLA Ops:
  0.6 94.6 %shard_map.144 = (bf16[256,512]{1,0:T(8,128)(2,1)}, bf16[256,512]{1,0:T(8,128)(2,1)}, bf16[2,2048,256]{2,1,0:T(8,128)(2,1)}) custom-call(s32[2,6]{1,0:T(2,128)} %near_ref.1, bf16[2,128,512]{2,1,0:T(8,128)(2,1)} %bitcast.8, f32[1,512]{1,0:T(1,128)} %bitcast.9, s32[2,128]{1,0:T(2,128)} %labels.1, bf16[512,512]{1,0:T(8,128)(2,1)} %wq.1, bf16[512,512]{1,0:T(8,128)(2,1)} %wk.1, ...), custom_call_target="tpu_custom_call" | custom-call | tf_op jit(solution)/shard_map/pallas_call | solution.py:598
  95.3 5.0 %shard_map.145 = (bf16[256,512]{1,0:T(8,128)(2,1)}, bf16[256,512]{1,0:T(8,128)(2,1)}, f32[512,512]{1,0:T(8,128)}, f32[512,512]{1,0:T(8,128)}, f32[512,512]{1,0:T...) custom-call(bf16[2,2,2,512,256]{4,3,2,1,0:T(8,128)(2,1)} %bitcast.4, bf16[2,2,2,512,256]{4,3,2,1,0:T(8,128)(2,1)} %bitcast.5, ...), custom_call_target="tpu_custom_call" | custom-call | tf_op jit(solution)/shard_map/pallas_call | solution.py:660

commit v4 on v3

--- a/solution.py
+++ b/solution.py
@@ -12,7 +12,7 @@
 EPSILON = 1e-05
 F32 = jnp.float32
 BF16 = jnp.bfloat16
-VMEM_LIMIT = 56 * 1024 * 1024
+VMEM_LIMIT = 58 * 1024 * 1024
 NN = (((1,), (0,)), ((), ()))
 NT = (((1,), (1,)), ((), ()))
 TN = (((0,), (0,)), ((), ()))
@@ -62,7 +62,7 @@
     near_ref, states, gain, labels, wq_hbm, wk_hbm, wv_hbm, wo_hbm, cot_hbm,
     branch, grad_states, summed,
     wq, wk, wv, wo, cot, marks, g, gl, far, fl, table,
-    normed, q_own, d_att, keys, normed_keys, values, key_marks, bias,
+    normed, packed, q_own, d_att, keys, normed_keys, values, key_marks, bias,
     q_wide, d_wide, scores, d_probs, probs, d_scores, att, dq, kv_grad,
     parts, far_two, far_parts, base_t,
     give, take, far_send, far_recv, near_send, near_recv, line,
@@ -99,6 +99,9 @@
     lax.fori_loop(1, 16, greet, 0)
     marks[...] = jnp.zeros((8, 128), jnp.int32)
     marks[:2] = labels[...]
+    gain_row = gain[...]
+    for k in range(2):
+        packed[k] = normalize(states[k], gain_row)
     pl.semaphore_wait(barrier, 19)
     started = []
 
@@ -121,11 +124,11 @@
             send(src, dst, as_.at[n], ar.at[n], to)
 
         def cross(i, j):
-            src = states if i == 0 and j == 0 else slot(i, j)
+            src = packed if i == 0 and j == 0 else slot(i, j)
             send(src, slot(i, j), mate_s.at[i * 4 + j], mate_r.at[i * 4 + j], mate)
 
         def second_out(i, half, way):
-            src = states if i == 0 else slot(i, 0)
+            src = packed if i == 0 else slot(i, 0)
             out(6 + 6 * i + 2 * way + half, src.at[half], slot(i, 0).at[half], b_to[2 - way])
 
         def second_in(i, half, way):
@@ -145,16 +148,16 @@
         for block in range(2):
             for way in range(2):
                 half = block if way == 0 else 1 - block
-                out(2 * way + half, states.at[half], slot(0, 0).at[half], a_to[2 - way])
+                out(2 * way + half, packed.at[half], slot(0, 0).at[half], a_to[2 - way])
             for way in range(2):
                 second_out(0, block if way == 0 else 1 - block, way)
         row = gl.at[c, b, a]
         send(marks, row, ls.at[0], lr.at[0], a_to[2])
         send(marks, row, ls.at[1], lr.at[1], a_to[1])
-        send(states, far, zs.at[0], zr.at[0], z_to[1])
+        send(packed, far, zs.at[0], zr.at[0], z_to[1])
         send(marks, fl, zs.at[1], zr.at[1], z_to[1])
         cross(0, 0)
-        g[c, b, a] = states[...]
+        g[c, b, a] = packed[...]
         gl[c, b, a] = marks[...]
         yield
         for way in range(2):
@@ -214,14 +217,12 @@
         got(gl.at[1 - c], ls.at[6], lr.at[6])
         yield
 
-    gain_row = gain[...]
-
     def own_rows():
         for n in range(3):
             loads[n].wait()
         for k in range(2):
             rows = slice(k * 128, (k + 1) * 128)
-            normed[rows] = normalize(states[k], gain_row)
+            normed[rows] = packed[k]
             normed_keys[k, :128] = normed[rows]
         q_own[...] = (dot(normed[...], wq[...]).astype(BF16) * 0.125).astype(BF16)
         d_att[...] = dot(cot[...], wo[...], NT).astype(BF16)
@@ -243,7 +244,7 @@
         got(fl, zs.at[1], zr.at[1])
         for k in range(2):
             m = lax.rem(near_ref[k, 5], 2)
-            normed_keys[k, 640:] = normalize(far[m], gain_row)
+            normed_keys[k, 640:] = far[m]
             project(k, slice(640, 768))
             key_marks[k, :, 640:] = jnp.broadcast_to(fl[pl.ds(m, 1)], (8, 128)).astype(F32)
 
@@ -269,7 +270,7 @@
         first, second = ax * (1 - core) + ay * core, ay * (1 - core) + ax * core
         local = lax.rem(block, 2)
         rows = slice((1 + e) * 128, (2 + e) * 128)
-        normed_keys[k, rows] = normalize(g[core, second, first, local], gain_row)
+        normed_keys[k, rows] = g[core, second, first, local]
         key_marks[k, :, rows] = jnp.broadcast_to(gl[core, second, first, pl.ds(local, 1)], (8, 128)).astype(F32)
 
     def fetched_keys():
@@ -291,16 +292,21 @@
 
     head_of = lax.broadcasted_iota(jnp.int32, (128, 256), 1) // 64
 
+    def widen():
+        for n in range(4):
+            rows, cols = slice(n // 2 * 128, n // 2 * 128 + 128), slice(n % 2 * 256, n % 2 * 256 + 256)
+            q_part, d_part = q_own[rows, cols].astype(F32), d_att[rows, cols].astype(F32)
+            for i in range(4):
+                at = slice(i * 128, (i + 1) * 128)
+                q_wide[n, at] = jnp.where(head_of == i, q_part, 0.0).astype(BF16)
+                d_wide[n, at] = jnp.where(head_of == i, d_part, 0.0).astype(BF16)
+
     def attend(n, _):
         k, half = lax.div(n, 2), lax.rem(n, 2)
         rows = pl.ds(pl.multiple_of(k * 128, 128), 128)
         cols = pl.ds(pl.multiple_of(half * 256, 256), 256)
-        for i in range(4):
-            at = slice(i * 128, (i + 1) * 128)
-            q_wide[at] = jnp.where(head_of == i, q_own[rows, cols].astype(F32), 0.0).astype(BF16)
-            d_wide[at] = jnp.where(head_of == i, d_att[rows, cols].astype(F32), 0.0).astype(BF16)
-        scores[...] = dot(q_wide[...], keys[k, :, cols], NT)
-        d_probs[...] = dot(d_wide[...], values[k, :, cols], NT)
+        scores[...] = dot(q_wide[n], keys[k, :, cols], NT)
+        d_probs[...] = dot(d_wide[n], values[k, :, cols], NT)
 
         def soft(t, _):
             at = pl.ds(pl.multiple_of(t * 128, 128), 128)
@@ -323,8 +329,8 @@
             two = two + jnp.where(head_of == i, turned[at], 0.0)
         att[rows, cols] = one.astype(BF16)
         dq[rows, cols] = (two * 0.125).astype(BF16)
-        kv_grad[k, cols] = dot(q_wide[...], d_scores[...], TN).astype(BF16)
-        kv_grad[k, pl.ds(pl.multiple_of(512 + half * 256, 256), 256)] = dot(d_wide[...], probs[...], TN).astype(BF16)
+        kv_grad[k, cols] = dot(q_wide[n], d_scores[...], TN).astype(BF16)
+        kv_grad[k, pl.ds(pl.multiple_of(512 + half * 256, 256), 256)] = dot(d_wide[n], probs[...], TN).astype(BF16)
         return 0
 
     def hold(p, m, value):
@@ -559,6 +565,7 @@
     plan_parts()
     next(states_in)
     far_keys()
+    widen()
     for _ in range(4):
         next(states_in)
     fetched_keys()
@@ -577,7 +584,7 @@
 
 
 AHEAD = 1
-PLAN = "QwKvN3wv12r0wrrEOwvrrvwrrrvrwrwvv"
+PLAN = "QwKvwN3v12r0wrrEwvrrOvwrrrvrwrwvv"
 
 
 def layer(neighbours, states, gain, labels, wq, wk, wv, wo, cot):
@@ -608,9 +615,9 @@
             half(512, 512), half(512, 512), half(512, 512), half(512, 512), half(256, 512),
             whole(8, 128), half(2, 4, 4, 2, 128, 512), whole(2, 4, 4, 8, 128), half(2, 128, 512), whole(8, 128),
             pltpu.SMEM((64,), jnp.int32),
-            half(256, 512), half(256, 512), half(256, 512),
+            half(256, 512), half(2, 128, 512), half(256, 512), half(256, 512),
             half(2, 768, 512), half(2, 768, 512), half(2, 768, 512), full(2, 8, 768), full(2, 128, 768),
-            half(512, 256), half(512, 256), full(512, 768), full(512, 768), half(512, 768), half(512, 768),
+            half(4, 512, 256), half(4, 512, 256), full(512, 768), full(512, 768), half(512, 768), half(512, 768),
             half(256, 512), half(256, 512), half(2, 1024, 768),
             half(9, 512, 128), half(2, 512, 128), half(2, 512, 128), full(512, 256),
             half(16, 2, 512, 128), half(16, 2, 512, 128),

time: 101 us -> 99 us (0.980)
  Pallas kernels: 99.6 us -> 98.1 us
    pallas_call x1, Pallas kernels: 94.6 us -> 93.1 us  [layer(): pl.pallas_call(layer_kernel, out_shape=(jax.ShapeDtypeStruct((256, 512),...]
where the time goes in v4:
time: 99 us; the launch traced here: 98.8 us
  Pallas kernels  98.1 us (99%)
    pallas_call x1, Pallas kernels, layer(): pl.pallas_call(layer_kernel, out_shape=(jax.ShapeDtypeStruct((256, 512),...  93.1 us
    pallas_call x1, Pallas kernels, finish(): pl.pallas_call(finish_kernel, grid=(4,), out_shape=(rows, rows, square, s...  5 us

profile of v4, /device:TPU:1, one launch (start us, length us, event | category | flops | bytes accessed | tf_op | source)
XLA Modules:
  0.0 98.8 jit_solution(17958539969720588568)
XLA Ops:
  0.6 93.1 %shard_map.144 = (bf16[256,512]{1,0:T(8,128)(2,1)}, bf16[256,512]{1,0:T(8,128)(2,1)}, bf16[2,2048,256]{2,1,0:T(8,128)(2,1)}) custom-call(s32[2,6]{1,0:T(2,128)} %near_ref.1, bf16[2,128,512]{2,1,0:T(8,128)(2,1)} %bitcast.8, f32[1,512]{1,0:T(1,128)} %bitcast.9, s32[2,128]{1,0:T(2,128)} %labels.1, bf16[512,512]{1,0:T(8,128)(2,1)} %wq.1, bf16[512,512]{1,0:T(8,128)(2,1)} %wk.1, ...), custom_call_target="tpu_custom_call" | custom-call | tf_op jit(solution)/shard_map/pallas_call | solution.py:605
  93.8 5.0 %shard_map.145 = (bf16[256,512]{1,0:T(8,128)(2,1)}, bf16[256,512]{1,0:T(8,128)(2,1)}, f32[512,512]{1,0:T(8,128)}, f32[512,512]{1,0:T(8,128)}, f32[512,512]{1,0:T...) custom-call(bf16[2,2,2,512,256]{4,3,2,1,0:T(8,128)(2,1)} %bitcast.4, bf16[2,2,2,512,256]{4,3,2,1,0:T(8,128)(2,1)} %bitcast.5, ...), custom_call_target="tpu_custom_call" | custom-call | tf_op jit(solution)/shard_map/pallas_call | solution.py:667
